TPU v7x, 256 devices: a whole 4x4x8 slice. The times are simulated.
256 devices in a mesh: seq: 64 (over y, z, core), head: 4 (over x).
Axes of the slice: x: 4, y: 4, z: 8, core: 2. Of those that a mesh axis runs over, the one named last changes fastest.
Arguments:
- x_in: bfloat16 [32768, 4096], P('seq', 'head'), may hold values from -160 to 160
- gate_in: bfloat16 [32768, 4096], P('seq', 'head'), may hold values from -6 to 6
- bc_in: bfloat16 [32768, 256], P('seq'), may hold values from -2.390625 to 2.390625
- step_in: float32 [32768, 64], P('seq', 'head'), may hold values from 0.005 to 0.05
- decay_code: int32 [2, 32768, 64], P(None, 'seq', 'head'), may hold values from 1 to 131072
- decay_rate: float32 [2, 64], P(None, 'head'), may hold values from 1.8310547e-06 to 0.012
- skip_gain: float32 [2, 64], P(None, 'head'), may hold values from 0.25 to 1.5
- norm_gain: float32 [4096], P('head'), may hold values from 0.1 to 1.9
- w_out: bfloat16 [4096, 4096], P('head', 'seq'), may hold values from -0.09375 to 0.09375
- resid_in: bfloat16 [32768, 4096], P('seq', 'head'), may hold values from -25 to 25
- resid_gain: float32 [4096], replicated, may hold values from 0.1 to 1.9
- w_in_x: bfloat16 [4096, 4096], P('seq', 'head'), may hold values from -1 to 1
- w_in_bc: bfloat16 [4096, 256], P('seq'), may hold values from -0.09375 to 0.09375
- w_in_dt: bfloat16 [4096, 64], P('seq', 'head'), may hold values from -0.09375 to 0.09375
- step_time_bias: float32 [64], P('head'), may hold values from -3 to -1
- conv_x: bfloat16 [4, 4096], P(None, 'head'), may hold values from -3 to 3
- conv_bc: bfloat16 [4, 256], replicated, may hold values from -3 to 3
Outputs:
- resid_out: bfloat16 [32768, 4096], P('seq', 'head')
- mixer_out: bfloat16 [32768, 4096], P('seq', 'head')
All inputs are finite; a program needn't handle non-finite values.
Results may differ from a plain program's by a relative error of at most 0.007.
Values may be sent and summed in bfloat16 or wider, within the bound.
A program may use at most 128 MiB of HBM per device.

v0:
```python
import functools

import jax
import jax.numpy as jnp
from jax import lax
from jax.experimental import pallas as pl
from jax.experimental.pallas import tpu as pltpu
from jax.sharding import PartitionSpec as P

CH = 64
GROUP = 256
F32 = jnp.float32
BF16 = jnp.bfloat16
NT = (((1,), (1,)), ((), ()))
VMEM = pl.BlockSpec(memory_space=pltpu.VMEM)
HALO = 16


def iota(shape, dim):
    return lax.broadcasted_iota(jnp.int32, shape, dim)


def exact_dot(a, b, dims=None):
    if dims is None:
        return jnp.dot(a, b, precision=lax.Precision.HIGHEST, preferred_element_type=F32)
    return lax.dot_general(a, b, dims, precision=lax.Precision.HIGHEST, preferred_element_type=F32)


def bdot(a, b, dims=None):
    if dims is None:
        return jnp.dot(a, b, preferred_element_type=F32)
    return lax.dot_general(a, b, dims, preferred_element_type=F32)


def split_two(v):
    hi = v.astype(BF16)
    return hi, (v - hi.astype(F32)).astype(BF16)


def spread(v, heads):
    width = heads * CH
    e = (iota((heads, width), 1) // CH == iota((heads, width), 0)).astype(BF16)
    hi, lo = split_two(v)
    return bdot(hi, e) + bdot(lo, e)


def lower(n):
    return iota((n, n), 0) >= iota((n, n), 1)


def states_body(x_ref, bc_ref, step_ref, code_ref, rate_ref, send_ref, st_ref, cum_ref):
    rows, heads = step_ref.shape
    blocks = rows // GROUP
    tri = lower(GROUP).astype(F32)
    totals = []
    state = None
    for b in range(blocks):
        r = pl.ds(b * GROUP, GROUP)
        decay = -jnp.minimum(code_ref[r, :].astype(F32) * rate_ref[...], 20.0)
        cum = exact_dot(tri, decay)
        cum_ref[r, :] = cum
        last = cum[GROUP - 1 : GROUP, :]
        weight = jnp.exp(last - cum) * step_ref[r, :]
        v = (x_ref[r, :].astype(F32) * spread(weight, heads)).astype(BF16)
        term = lax.dot_general(
            bc_ref[r, : bc_ref.shape[1] // 2], v, (((0,), (0,)), ((), ())), preferred_element_type=F32
        )
        if state is None:
            state = term
            st_ref[...] = term
        else:
            factor = spread(jnp.broadcast_to(jnp.exp(last), (8, heads)), heads)[0:1]
            state = factor * state + term
        totals.append(last)
    half = state.shape[0] // 2
    width = state.shape[1]
    send_ref[:, :width] = state[:half].astype(BF16)
    send_ref[:, width : 2 * width] = state[half:].astype(BF16)
    total = sum(totals[1:], totals[0])
    pieces = []
    rest = total
    for _ in range(3):
        piece = rest.astype(BF16).astype(F32)
        pieces.append(piece)
        rest = rest - piece
    pieces.append(jnp.zeros((1, 128 - 3 * heads), F32))
    tail = jnp.concatenate(pieces, axis=1)
    send_ref[:, 2 * width :] = jnp.broadcast_to(tail, (half, 128)).astype(BF16)


def scan_body(heads, got_ref, out_ref, s_ref, d_ref, p_ref):
    count = got_ref.shape[0]
    width = heads * CH
    s_ref[...] = got_ref[:, : 2 * width].astype(F32)
    tail = got_ref[:, 2 * width :].astype(F32)
    total = tail[:, :heads] + tail[:, heads : 2 * heads] + tail[:, 2 * heads : 3 * heads]
    d = spread(jnp.exp(total), heads)
    d_ref[:, :width] = d
    d_ref[:, width:] = d

    def one(k, p):
        row = pl.ds(k, 1)
        p_ref[row, :] = p
        return d_ref[row, :] * p + s_ref[row, :]

    lax.fori_loop(0, count, one, jnp.zeros((1, 2 * width), F32))
    out_ref[...] = p_ref[...].astype(BF16)


def diag_body(x_ref, bc_ref, step_ref, cum_ref, skip_ref, y_ref):
    rows, heads = step_ref.shape
    n = bc_ref.shape[1] // 2
    half = GROUP // 2
    eye = (iota((heads, heads), 0) == iota((heads, heads), 1)).astype(F32)
    left = iota((GROUP, 2 * CH), 1) < CH
    skip = spread(jnp.broadcast_to(skip_ref[...], (8, heads)), heads)[0:1]
    zero = jnp.zeros((), BF16)
    for b in range(rows // GROUP):
        r = pl.ds(b * GROUP, GROUP)
        scores = bdot(bc_ref[r, n:], bc_ref[r, :n], NT)
        scores = jnp.where(lower(GROUP), scores, 0.0)
        cum = cum_ref[r, :]
        cum_row = exact_dot(eye, cum, NT)
        step_row = exact_dot(eye, step_ref[r, :], NT)
        for pair in range(heads // 2):
            lanes = pl.ds(pair * 2 * CH, 2 * CH)
            xp = x_ref[r, lanes]
            tops, bottoms = [], []
            for side in range(2):
                h = 2 * pair + side
                mine = jnp.where(left if side == 0 else ~left, xp, zero)
                col = cum[:, h : h + 1]
                row = cum_row[h : h + 1, :]
                srow = step_row[h : h + 1, :]
                top = (
                    jnp.exp(jnp.minimum(col[:half] - row[:, :half], 0.0))
                    * scores[:half, :half]
                    * srow[:, :half]
                ).astype(BF16)
                bottom = (
                    jnp.exp(jnp.minimum(col[half:] - row, 0.0)) * scores[half:, :] * srow
                ).astype(BF16)
                tops.append(bdot(top, mine[:half]))
                bottoms.append(bdot(bottom, mine))
            xs = xp.astype(F32) * skip[:, pair * 2 * CH : (pair + 1) * 2 * CH]
            y_ref[pl.ds(b * GROUP, half), lanes] = tops[0] + tops[1] + xs[:half]
            y_ref[pl.ds(b * GROUP + half, half), lanes] = bottoms[0] + bottoms[1] + xs[half:]


def mixed_blocks(bc_ref, cum_ref, prev_ref, st_ref, y_ref):
    rows, heads = cum_ref.shape
    width = heads * CH
    n = bc_ref.shape[1] // 2
    out = []
    low = high = None
    for b in range(rows // GROUP):
        r = pl.ds(b * GROUP, GROUP)
        c = bc_ref[r, n:]
        cum = cum_ref[r, :]
        if b == 0:
            high = jnp.concatenate([prev_ref[:, :width], prev_ref[:, width:]], axis=0)
            inner = bdot(c, high)
        else:
            last = cum_ref[pl.ds(GROUP - 8, 8), :]
            factor = spread(jnp.exp(last), heads)[7:8]
            state = factor * high.astype(F32) + st_ref[...]
            hi, lo = split_two(state)
            inner = bdot(c, hi) + bdot(c, lo)
        out.append((r, y_ref[r, :] + inner * spread(jnp.exp(cum), heads)))
    return out


def gate_body(bc_ref, cum_ref, prev_ref, st_ref, y_ref, gate_ref, gain_ref, g_ref, ss_ref):
    ones = jnp.ones((8, g_ref.shape[1]), F32)
    for r, mixed in mixed_blocks(bc_ref, cum_ref, prev_ref, st_ref, y_ref):
        gate = gate_ref[r, :].astype(F32)
        gated = mixed * (gate / (1.0 + jnp.exp(-gate)))
        g_ref[r, :] = (gated * gain_ref[...]).astype(BF16)
        ss_ref[:, r] = exact_dot(ones, gated * gated, NT)


def last_body(bc_ref, cum_ref, prev_ref, st_ref, y_ref, m_ref, ss_ref):
    ones = jnp.ones((8, m_ref.shape[1]), F32)
    for r, mixed in mixed_blocks(bc_ref, cum_ref, prev_ref, st_ref, y_ref):
        m_ref[r, :] = mixed
        ss_ref[:, r] = exact_dot(ones, mixed * mixed, NT)


def second_body(
    hid_ref, halo_ref, gain_ref, w_ref, bias_ref, cx_ref, cbc_ref, x_ref, bc_ref, step_ref, h_ref, pre_ref, rs_ref
):
    rows, depth = hid_ref.shape
    width = x_ref.shape[1]
    heads = step_ref.shape[1]
    states = bc_ref.shape[1]
    first = lax.axis_index("seq") == 0

    def scaled(src, r, at, n, keep):
        v = src[r, :].astype(F32)
        rs = lax.rsqrt(jnp.sum(v * v, axis=1, keepdims=True) / depth + 1e-05)
        rs_ref[pl.ds(at, n), :] = jnp.broadcast_to(rs if keep is None else rs * keep, (n, 128))
        h_ref[pl.ds(at, n), :] = (v * gain_ref[...]).astype(BF16)

    scaled(halo_ref, pl.ds(0, HALO), 0, HALO, jnp.where(first, 0.0, 1.0))
    step = 64

    @pl.loop(0, rows // step)
    def _(i):
        at = pl.multiple_of(i * step, step)
        scaled(hid_ref, pl.ds(at, step), pl.multiple_of(at + HALO, 16), step, None)

    def project(cols):
        return bdot(h_ref[...], w_ref[:, cols])

    def conv(taps, k):
        n = taps.shape[1]
        total = None
        for tap in range(k):
            v = pre_ref[pl.ds(HALO - k + 1 + tap, rows), :n] * taps[tap : tap + 1, :].astype(F32)
            total = v if total is None else total + v
        return (total / (1.0 + jnp.exp(-total))).astype(BF16)

    tile = 256
    rs_all = rs_ref[...]
    rs2 = jnp.concatenate([rs_all, rs_all], axis=1)

    @pl.loop(0, width // tile)
    def _(i):
        at = pl.multiple_of(i * tile, tile)
        cols = pl.ds(at, tile)
        pre_ref[...] = (project(cols) * rs2).astype(BF16).astype(F32)
        x_ref[:, cols] = conv(cx_ref[:, cols], cx_ref.shape[0])

    pre_ref[...] = (project(pl.ds(width, states)) * rs2).astype(BF16).astype(F32)
    bc_ref[...] = conv(cbc_ref[...], cbc_ref.shape[0])
    dt = bdot(h_ref[pl.ds(HALO, rows), :], w_ref[:, pl.ds(width + states, 128)])
    dt = (dt * rs_ref[pl.ds(HALO, rows), :])[:, :heads] + bias_ref[...]
    step_ref[...] = jnp.maximum(dt, 0.0) + jnp.log(1.0 + jnp.exp(-jnp.abs(dt)))


def call(body, outs, args, scratch=(), limit=56, **kw):
    return pl.pallas_call(
        body,
        out_shape=outs,
        in_specs=[VMEM] * len(args),
        out_specs=jax.tree.map(lambda _: VMEM, outs),
        scratch_shapes=list(scratch),
        compiler_params=pltpu.CompilerParams(vmem_limit_bytes=limit * 2**20, **kw),
    )(*args)


def sds(*shape, dtype=F32):
    return jax.ShapeDtypeStruct(shape, dtype)


def prefix(send, heads):
    count, wide = send.shape
    got = lax.all_to_all(send, "seq", 0, 0, tiled=True)
    width = wide - 128
    back = call(
        functools.partial(scan_body, heads),
        sds(count, width, dtype=BF16),
        (got,),
        [pltpu.VMEM((count, width), F32) for _ in range(3)],
    )
    return lax.all_to_all(back, "seq", 0, 0, tiled=True)


def local_states(x, bc, step, code, rate):
    rows, heads = step.shape
    n = bc.shape[1] // 2
    width = heads * CH
    return call(
        states_body,
        (sds(n // 2, 2 * width + 128, dtype=BF16), sds(n, width), sds(rows, heads)),
        (x, bc, step, code, rate),
    )


def diagonal(x, bc, step, cum, skip):
    return call(diag_body, sds(*x.shape), (x, bc, step, cum, skip))


def on_device(
    x_in, gate_in, bc_in, step_in, decay_code, decay_rate, skip_gain, norm_gain, w_out, resid_in,
    resid_gain, w_in_x, w_in_bc, w_in_dt, step_time_bias, conv_x, conv_bc,
):
    rows, width = x_in.shape
    heads = step_in.shape[1]
    inner = width * lax.axis_size("head")
    w_out_all = lax.all_gather(w_out, "seq", axis=1, tiled=True)
    w_in = jnp.concatenate(
        [w_in_x, w_in_bc, jnp.pad(w_in_dt, ((0, 0), (0, 128 - heads)))], axis=1
    )
    w_in_all = lax.all_gather(w_in, "seq", axis=0, tiled=True)

    send, st, cum = local_states(x_in, bc_in, step_in, decay_code[0], decay_rate[0:1])
    y = diagonal(x_in, bc_in, step_in, cum, skip_gain[0:1])
    prev = prefix(send, heads)
    g, ss = call(
        gate_body,
        (sds(rows, width, dtype=BF16), sds(8, rows)),
        (bc_in, cum, prev, st, y, gate_in, norm_gain[None, :]),
    )
    rs = lax.rsqrt(lax.psum(ss[0], "head") / inner + 1e-05)
    projected = jnp.dot(g, w_out_all, preferred_element_type=F32).astype(BF16)
    share = lax.psum_scatter(projected, "head", scatter_dimension=1, tiled=True)
    resid_out = (resid_in.astype(F32) + share.astype(F32) * rs[:, None]).astype(BF16)
    hidden = lax.all_gather(resid_out, "head", axis=1, tiled=True)
    size = lax.axis_size("seq")
    halo = lax.ppermute(hidden[rows - HALO :], "seq", [(i, i + 1) for i in range(size - 1)])

    x_two, bc_two, step_two = call(
        second_body,
        (sds(rows, width, dtype=BF16), sds(*bc_in.shape, dtype=BF16), sds(rows, heads)),
        (hidden, halo, resid_gain[None, :], w_in_all, step_time_bias[None, :], conv_x, conv_bc),
        [
            pltpu.VMEM((rows + HALO, inner), BF16),
            pltpu.VMEM((rows + HALO, 256), F32),
            pltpu.VMEM((rows + HALO, 128), F32),
        ],
    )
    send, st, cum = local_states(x_two, bc_two, step_two, decay_code[1], decay_rate[1:2])
    y = diagonal(x_two, bc_two, step_two, cum, skip_gain[1:2])
    prev = prefix(send, heads)
    mixed, ss = call(last_body, (sds(rows, width), sds(8, rows)), (bc_two, cum, prev, st, y))
    rs = lax.rsqrt(lax.psum(ss[0], "head") / inner + 1e-05)
    return resid_out, (mixed * rs[:, None]).astype(BF16)


def solution(mesh):
    in_specs = (
        P("seq", "head"), P("seq", "head"), P("seq", None), P("seq", "head"), P(None, "seq", "head"),
        P(None, "head"), P(None, "head"), P("head"), P("head", "seq"), P("seq", "head"), P(),
        P("seq", "head"), P("seq", None), P("seq", "head"), P("head"), P(None, "head"), P(),
    )
    out_specs = (P("seq", "head"), P("seq", "head"))
    return jax.shard_map(
        on_device, mesh=mesh, in_specs=in_specs, out_specs=out_specs, check_vma=False
    )
```

profile of v0, /device:TPU:1, one launch (start us, length us, event | category | flops | bytes accessed | tf_op | source)
XLA Modules:
  0.0 394.9 jit_solution(2149528970205686691)
XLA Ops:
  7.2 0.0 all-gather.4.cloned.1.call-start
  7.2 0.7 all-gather.4.cloned.1.call-update
  7.9 0.8 fusion.2
  8.7 0.9 copy.46
  9.6 1.6 copy.34.step_ref
  11.2 1.3 fusion.4
  12.5 4.7 %shard_map.176 = (bf16[64,2176]{1,0:T(8,128)(2,1)}, f32[128,1024]{1,0:T(8,128)}, f32[512,16]{1,0:T(8,128)}) custom-call(bf16[512,1024]{1,0:T(8,128)(2,1)} %x_ref.3, bf16[512,256]{1,0:T(8,128)(2,1)} %bc_ref.5, f32[512,16]{1,0:T(8,128)} %copy.34.step_ref, s32[512,16]{1,0:T(8,128)} %bitcast.31, f32[1,16]{1,0:T(1,128)} %get-tuple-element.33.rate_ref), custom_call_target="tpu_custom_call" | custom-call | tf_op jit(solution)/shard_map/pallas_call | solution.py:242
  17.2 0.5 broadcast.22
  17.8 1.7 reduce
  19.4 0.3 reshape.14
  19.7 0.0 copy-start.5
  19.8 27.1 %all_to_all.44 = bf16[64,2,1088]{2,1,0:T(2,128)(2,1)S(1)} all-to-all(bf16[64,2,1088]{2,1,0:T(2,128)(2,1)S(1)} %reshape.14), channel_id=1, replica_groups=mesh['seq'=64,'head'=4] {'seq'}, dimensions={0} | all-to-all | bytes 557056 | tf_op jit(solution)/shard_map/all_to_all | solution.py:258
  46.8 0.3 reshape.15
  47.2 0.7 copy.53
  47.9 2.6 shard_map.177
  50.5 1.7 reduce.1
  52.2 0.9 reshape.16
  53.1 6.2 %all-to-all-start.1 = ((bf16[64,2,1024]{2,1,0:T(2,128)(2,1)}), bf16[64,2,1024]{2,1,0:T(2,128)(2,1)S(1)}, u32[]{:S(2)}, u32[]{:S(2)}) async-start(bf16[64,2,1024]{2,1,0:T(2,128)(2,1)} %reshape.16), calls=%async_computation.1 | async-start | bytes 524288 | tf_op jit(solution)/shard_map/all_to_all | solution.py:266
  59.3 0.2 reduce-scatter.2.cloned.1.call-start
  59.6 0.5 fusion.3
  60.1 5.8 %shard_map.178.y_ref = f32[512,1024]{1,0:T(8,128)} custom-call(bf16[512,1024]{1,0:T(8,128)(2,1)} %x_ref.3, bf16[512,256]{1,0:T(8,128)(2,1)} %bc_ref.5, f32[512,16]{1,0:T(8,128)} %copy.34.step_ref, f32[512,16]{1,0:T(8,128)} %get-tuple-element.15.cum_ref, f32[1,16]{1,0:T(1,128)} %get-tuple-element.31.skip_ref), custom_call_target="tpu_custom_call" | custom-call | tf_op jit(solution)/shard_map/pallas_call | solution.py:242
  65.9 5.4 %all-to-all-done.1 = bf16[64,2,1024]{2,1,0:T(2,128)(2,1)S(1)} async-done(((bf16[64,2,1024]{2,1,0:T(2,128)(2,1)}), bf16[64,2,1024]{2,1,0:T(2,128)(2,1)S(1)}, u32[]{:S(2)}, u32[]{:S(2)}) %all-to-all-start.1) | async-done | bytes 262176 | tf_op jit(solution)/shard_map/all_to_all | solution.py:266
  71.3 0.2 reshape.17
  71.6 0.9 copy.55
  72.4 6.6 %shard_map.179 = (bf16[512,1024]{1,0:T(8,128)(2,1)}, f32[8,512]{1,0:T(8,128)}) custom-call(bf16[512,256]{1,0:T(8,128)(2,1)} %bc_ref.5, f32[512,16]{1,0:T(8,128)} %get-tuple-element.15.cum_ref, bf16[64,2048]{1,0:T(8,128)(2,1)} %bitcast.27, f32[128,1024]{1,0:T(8,128)} %get-tuple-element.17.st_ref, f32[512,1024]{1,0:T(8,128)} %shard_map.178.y_ref, ...), custom_call_target="tpu_custom_call" | custom-call | tf_op jit(solution)/shard_map/pallas_call | solution.py:242
  79.0 20.0 %all-gather.4.cloned.1.call-done = bf16[1024,4096]{0,1:T(8,128)(2,1)} async-done(((bf16[1024,64]{0,1:T(8,128)(2,1)}), bf16[1024,4096]{0,1:T(8,128)(2,1)}) %all-gather.4.cloned.1.call-update) | async-done | bytes 8388624 | tf_op jit(solution)/shard_map/all_gather | solution.py:291
  99.0 10.2 %convolution_convert_fusion = bf16[512,4096]{1,0:T(8,128)(2,1)} fusion(bf16[512,1024]{1,0:T(8,128)(2,1)} %get-tuple-element.18, bf16[1024,4096]{0,1:T(8,128)(2,1)} %all-gather.4.cloned.1.call-done), kind=kOutput, calls=%fused_computation | convolution fusion | flops 4297064448 | bytes 13631488 | tf_op jit(solution)/shard_map/dot_general | solution.py:306
  109.2 0.0 reduce-scatter.2.cloned.1.call-update
  109.3 0.0 all-gather.6.cloned.1.call-start
  109.3 0.8 slice.30
  110.1 8.9 %psum.14 = f32[512]{0:T(512)S(1)} all-reduce(f32[512]{0:T(512)S(1)} %bitcast.36), channel_id=1, replica_groups=mesh['seq'=64,'head'=4] {'head'}, use_global_device_ids=true, to_apply=%region_1.2 | all-reduce | flops 512 | bytes 4096 | tf_op jit(solution)/shard_map/psum | solution.py:305
  119.0 0.0 copy-start.3
  119.0 37.4 %reduce-scatter.2.cloned.1.call-done = bf16[512,1024]{1,0:T(8,128)(2,1)} async-done(((bf16[512,4096]{1,0:T(8,128)(2,1)}), bf16[512,1024]{1,0:T(8,128)(2,1)}) %reduce-scatter.2.cloned.1.call-update) | async-done | bytes 1048592 | tf_op jit(solution)/shard_map/reduce_scatter | solution.py:307
  156.4 2.6 add_convert_fusion
  159.0 0.0 all-gather.6.cloned.1.call-update
  159.0 0.0 all-gather.8.cloned.1.call-start
  159.1 0.1 copy.38
  159.2 0.7 fusion.1
  159.9 0.0 all-gather.8.cloned.1.call-update
  159.9 49.8 %all-gather.6.cloned.1.call-done.hid_ref = bf16[512,4096]{1,0:T(8,128)(2,1)} async-done(((bf16[512,1024]{1,0:T(8,128)(2,1)}), bf16[512,4096]{1,0:T(8,128)(2,1)}) %all-gather.6.cloned.1.call-update) | async-done | bytes 4194320 | tf_op jit(solution)/shard_map/all_gather | solution.py:309
  209.6 0.9 slice.36
  210.5 4.0 %collective-permute-start = (bf16[16,4096]{1,0:T(8,128)(2,1)S(1)}, bf16[16,4096]{1,0:T(8,128)(2,1)S(1)}, u32[]{:S(2)}, u32[]{:S(2)}) collective-permute-start(bf16[16,4096]{1,0:T(8,128)(2,1)S(1)} %slice.36), channel_id=1, source_target_pairs={{0,4},{4,8},{8,12},{12,16},{16,20},{20,24},{24,28},{28,32},{32,36}... | collective-permute-start | bytes 393224 | tf_op jit(solution)/shard_map/ppermute | solution.py:311
  214.6 0.8 copy.47
  215.4 86.6 %all-gather.8.cloned.1.call-done.w_ref = bf16[4096,1408]{1,0:T(8,128)(2,1)} async-done(((bf16[64,1408]{1,0:T(8,128)(2,1)}), bf16[4096,1408]{1,0:T(8,128)(2,1)}) %all-gather.8.cloned.1.call-update) | async-done | bytes 11534352 | tf_op jit(solution)/shard_map/all_gather | solution.py:295
  302.0 0.7 copy-done.1
  302.7 17.9 %shard_map.180 = (bf16[512,1024]{1,0:T(8,128)(2,1)}, bf16[512,256]{1,0:T(8,128)(2,1)}, f32[512,16]{1,0:T(8,128)}) custom-call(bf16[512,4096]{1,0:T(8,128)(2,1)} %all-gather.6.cloned.1.call-done.hid_ref, bf16[16,4096]{1,0:T(8,128)(2,1)} %copy-done.1, f32[1,4096]{1,0:T(1,128)} %bitcast.35, bf16[4096,1408]{1,0:T(8,128)(2,1)} %all-gather.8.cloned.1.call-done.w_ref, ...), custom_call_target="tpu_custom_call" | custom-call | tf_op jit(solution)/shard_map/pallas_call | solution.py:242
  320.6 4.7 %shard_map.181 = (bf16[64,2176]{1,0:T(8,128)(2,1)}, f32[128,1024]{1,0:T(8,128)}, f32[512,16]{1,0:T(8,128)}) custom-call(bf16[512,1024]{1,0:T(8,128)(2,1)} %get-tuple-element.21.x_ref, bf16[512,256]{1,0:T(8,128)(2,1)} %get-tuple-element.20.bc_ref, f32[512,16]{1,0:T(8,128)} %get-tuple-element.22.step_ref, s32[512,16]{1,0:T(8,128)} %bitcast.30, ...), custom_call_target="tpu_custom_call" | custom-call | tf_op jit(solution)/shard_map/pallas_call | solution.py:242
  325.3 1.7 reduce.2
  327.0 0.3 reshape.18
  327.3 18.2 %all_to_all.45 = bf16[64,2,1088]{2,1,0:T(2,128)(2,1)S(1)} all-to-all(bf16[64,2,1088]{2,1,0:T(2,128)(2,1)S(1)} %reshape.18), channel_id=1, replica_groups=mesh['seq'=64,'head'=4] {'seq'}, dimensions={0} | all-to-all | bytes 557056 | tf_op jit(solution)/shard_map/all_to_all | solution.py:258
  345.5 0.3 reshape.19
  345.8 0.7 copy.52
  346.6 2.5 shard_map.182
  349.1 1.7 reduce.3
  350.8 0.9 reshape.20
  351.7 6.1 %all-to-all-start.3 = ((bf16[64,2,1024]{2,1,0:T(2,128)(2,1)}), bf16[64,2,1024]{2,1,0:T(2,128)(2,1)S(1)}, u32[]{:S(2)}, u32[]{:S(2)}) async-start(bf16[64,2,1024]{2,1,0:T(2,128)(2,1)} %reshape.20), calls=%async_computation.4 | async-start | bytes 524288 | tf_op jit(solution)/shard_map/all_to_all | solution.py:266
  357.8 5.8 %shard_map.183.y_ref = f32[512,1024]{1,0:T(8,128)} custom-call(bf16[512,1024]{1,0:T(8,128)(2,1)} %get-tuple-element.21.x_ref, bf16[512,256]{1,0:T(8,128)(2,1)} %get-tuple-element.20.bc_ref, f32[512,16]{1,0:T(8,128)} %get-tuple-element.22.step_ref, f32[512,16]{1,0:T(8,128)} %get-tuple-element.23.cum_ref, f32[1,16]{1,0:T(1,128)} %get-tuple-element.30.skip_ref), custom_call_target="tpu_custom_call" | custom-call | tf_op jit(solution)/shard_map/pallas_call | solution.py:242
  363.5 6.2 %all-to-all-done.3 = bf16[64,2,1024]{2,1,0:T(2,128)(2,1)S(1)} async-done(((bf16[64,2,1024]{2,1,0:T(2,128)(2,1)}), bf16[64,2,1024]{2,1,0:T(2,128)(2,1)S(1)}, u32[]{:S(2)}, u32[]{:S(2)}) %all-to-all-start.3) | async-done | bytes 262176 | tf_op jit(solution)/shard_map/all_to_all | solution.py:266
  369.8 0.2 reshape.21
  370.0 0.9 copy.54
  370.9 5.6 %shard_map.184 = (f32[512,1024]{1,0:T(8,128)}, f32[8,512]{1,0:T(8,128)}) custom-call(bf16[512,256]{1,0:T(8,128)(2,1)} %get-tuple-element.20.bc_ref, f32[512,16]{1,0:T(8,128)} %get-tuple-element.23.cum_ref, bf16[64,2048]{1,0:T(8,128)(2,1)} %bitcast.32, f32[128,1024]{1,0:T(8,128)} %get-tuple-element.25.st_ref, f32[512,1024]{1,0:T(8,128)} %shard_map.183.y_ref), custom_call_target="tpu_custom_call" | custom-call | tf_op jit(solution)/shard_map/pallas_call | solution.py:242
  376.5 0.7 slice.35
  377.2 8.4 %psum.15 = f32[512]{0:T(512)S(1)} all-reduce(f32[512]{0:T(512)S(1)} %bitcast.37), channel_id=1, replica_groups=mesh['seq'=64,'head'=4] {'head'}, use_global_device_ids=true, to_apply=%region_2.3 | all-reduce | flops 512 | bytes 4096 | tf_op jit(solution)/shard_map/psum | solution.py:327
  385.6 2.7 multiply_convert_fusion
  (12 shorter events, 0.0 us)
Async XLA Ops:
  7.2 91.9 %all-gather.4.cloned.1.call-start = ((), (), s32[]{:S(2)}) async-start(), calls=%async_computation.5 | async-start | bytes 8519680 | tf_op jit(solution)/shard_map/all_gather | solution.py:291
  19.7 39.8 %copy-start.5 = (f32[2,16]{1,0:T(2,128)S(1)}, f32[2,16]{1,0:T(2,128)}, u32[]{:S(2)}) copy-start(f32[2,16]{1,0:T(2,128)} %param.23) | copy-start | bytes 388
  53.1 18.2 %all-to-all-start.1 = ((bf16[64,2,1024]{2,1,0:T(2,128)(2,1)}), bf16[64,2,1024]{2,1,0:T(2,128)(2,1)S(1)}, u32[]{:S(2)}, u32[]{:S(2)}) async-start(bf16[64,2,1024]{2,1,0:T(2,128)(2,1)} %reshape.16), calls=%async_computation.1 | async-start | bytes 524288 | tf_op jit(solution)/shard_map/all_to_all | solution.py:266
  59.3 97.1 %reduce-scatter.2.cloned.1.call-start = ((), (), s32[]{:S(2)}) async-start(), calls=%async_computation.6 | async-start | bytes 5242880 | tf_op jit(solution)/shard_map/reduce_scatter | solution.py:307
  109.2 47.2 %copy-start = (bf16[512,1024]{1,0:T(8,128)(2,1)S(1)}, bf16[512,1024]{1,0:T(8,128)(2,1)}, u32[]{:S(2)}) copy-start(bf16[512,1024]{1,0:T(8,128)(2,1)} %param.26) | copy-start | bytes 3145732
  109.3 100.4 %all-gather.6.cloned.1.call-start = ((), (), s32[]{:S(2)}) async-start(), calls=%async_computation.7 | async-start | bytes 5242880 | tf_op jit(solution)/shard_map/all_gather | solution.py:309
  119.0 40.0 %copy-start.4 = (bf16[64,16]{0,1:T(8,128)(2,1)S(1)}, bf16[64,16]{0,1:T(8,128)(2,1)}, u32[]{:S(2)}) copy-start(bf16[64,16]{0,1:T(8,128)(2,1)} %param.30) | copy-start | bytes 6148
  119.0 40.1 %copy-start.2 = (bf16[64,1024]{1,0:T(8,128)(2,1)S(1)}, bf16[64,1024]{1,0:T(8,128)(2,1)}, u32[]{:S(2)}) copy-start(bf16[64,1024]{1,0:T(8,128)(2,1)} %param.28) | copy-start | bytes 393220
  119.0 40.1 %copy-start.3 = (bf16[64,256]{1,0:T(8,128)(2,1)S(1)}, bf16[64,256]{1,0:T(8,128)(2,1)}, u32[]{:S(2)}) copy-start(bf16[64,256]{1,0:T(8,128)(2,1)} %param.29) | copy-start | bytes 98308
  159.0 143.0 %all-gather.8.cloned.1.call-start = ((), (), s32[]{:S(2)}) async-start(), calls=%async_computation.8 | async-start | bytes 11714560 | tf_op jit(solution)/shard_map/all_gather | solution.py:295
  210.5 91.5 %collective-permute-start = (bf16[16,4096]{1,0:T(8,128)(2,1)S(1)}, bf16[16,4096]{1,0:T(8,128)(2,1)S(1)}, u32[]{:S(2)}, u32[]{:S(2)}) collective-permute-start(bf16[16,4096]{1,0:T(8,128)(2,1)S(1)} %slice.36), channel_id=1, source_target_pairs={{0,4},{4,8},{8,12},{12,16},{16,20},{20,24},{24,28},{28,32},{32,36}... | collective-permute-start | bytes 393224 | tf_op jit(solution)/shard_map/ppermute | solution.py:311
  302.0 0.7 copy-start.1
  351.7 18.1 %all-to-all-start.3 = ((bf16[64,2,1024]{2,1,0:T(2,128)(2,1)}), bf16[64,2,1024]{2,1,0:T(2,128)(2,1)S(1)}, u32[]{:S(2)}, u32[]{:S(2)}) async-start(bf16[64,2,1024]{2,1,0:T(2,128)(2,1)} %reshape.20), calls=%async_computation.4 | async-start | bytes 524288 | tf_op jit(solution)/shard_map/all_to_all | solution.py:266
Sparse Core Ops, SparseCore 0:
  10.8 88.1 all-gather.3
  109.4 46.9 reduce-scatter.1
  159.1 50.4 all-gather.5
  213.2 88.8 all-gather.7
where the time goes:
time: 396 us; the launch traced here: 395 us
  waiting for transfers between devices  206 us (52%)
  blocking collectives  62.5 us (16%)
  Pallas kernels  56.2 us (14%)
  starting transfers between devices  16.7 us (4%)
  local copies, waits for them, and re-layouts  16.4 us (4%)
  between operations  13.9 us (4%)
  other arithmetic  12.8 us (3%)
  matrix products  10.2 us (3%)
    all_gather x1, waiting for transfers between devices, on_device(): w_in_all = lax.all_gather(w_in, 'seq', axis=0, tiled=True)  86.6 us
    pallas_call x9, Pallas kernels, call(): pl.pallas_call(body, out_shape=outs, in_specs=[VMEM] * len(args), out_spe...  56.2 us
    all_gather x1, waiting for transfers between devices, on_device(): hidden = lax.all_gather(resid_out, 'head', axis=1, tiled=True)  49.8 us
    all_to_all x2, blocking collectives, prefix(): got = lax.all_to_all(send, 'seq', 0, 0, tiled=True)  45.2 us
    reduce_scatter x1, waiting for transfers between devices, on_device(): share = lax.psum_scatter(projected, 'head', scatter_dimension=1, tiled=True)  37.4 us
    all_gather x1, waiting for transfers between devices, on_device(): w_out_all = lax.all_gather(w_out, 'seq', axis=1, tiled=True)  20 us
    psum x2, blocking collectives, on_device(): rs = lax.rsqrt(lax.psum(ss[0], 'head') / inner + 1e-05)  17.3 us
    all_to_all x2, starting transfers between devices, prefix(): return lax.all_to_all(back, 'seq', 0, 0, tiled=True)  12.3 us
  transfers between devices with their start and end apart: 7, of which 6 were waited for; matrix products, arithmetic and copies ran while one was open for 4% of the time, Pallas kernels for 6%

commit v1 on v0

--- a/solution.py
+++ b/solution.py
@@ -186,31 +186,306 @@
         ss_ref[:, r] = exact_dot(ones, mixed * mixed, NT)
 
 
-def second_body(
-    hid_ref, halo_ref, gain_ref, w_ref, bias_ref, cx_ref, cbc_ref, x_ref, bc_ref, step_ref, h_ref, pre_ref, rs_ref
+NC = 8
+CHUNK_LAG = 2
+MESH = pl.DeviceIdType.MESH
+Y, Z, CORES = 4, 8, 2
+
+
+def place():
+    seq = lax.axis_index("seq")
+    return seq // (Z * CORES), (seq // CORES) % Z, seq % CORES
+
+
+def seq_of(y, z, c):
+    return (y * Z + z) * CORES + c
+
+
+class Copies:
+    def __init__(self, send_sem, recv_sem):
+        self.send_sem, self.recv_sem = send_sem, recv_sem
+        self.names = {}
+        self.started = []
+
+    def _make(self, name, src, dst, device):
+        at = self.names.setdefault(name, len(self.names))
+        return pltpu.make_async_remote_copy(
+            src_ref=src, dst_ref=dst, send_sem=self.send_sem.at[at], recv_sem=self.recv_sem.at[at],
+            device_id=device, device_id_type=MESH,
+        )
+
+    def send(self, name, src, dst, device):
+        copy = self._make(name, src, dst, device)
+        copy.start()
+        self.started.append(copy)
+
+    def arrived(self, name, where, device):
+        self._make(name, where, where, device).wait_recv()
+
+    def finish(self):
+        for copy in self.started:
+            copy.wait_send()
+
+
+def weight_steps(cp, own, w, local_sem):
+    y, z, c = place()
+    head = lax.axis_index("head")
+    half = own.shape[0] // 2
+    f = 1 - 2 * c
+    top, low = pl.ds(0, half), pl.ds(half, half)
+
+    def at_y(k):
+        return lax.rem(y + k * f + 2 * Y, Y)
+
+    def at_z(k):
+        return lax.rem(z + k * f + 2 * Z, Z)
+
+    to_y = {k: (seq_of(at_y(k), z, c), head) for k in (1, -1)}
+    to_z = {k: (seq_of(y, at_z(k), c), head) for k in (1, -1)}
+    other = (seq_of(y, z, 1 - c), head)
+
+    def a_piece(ky):
+        return w.at[at_y(ky), z, c, top]
+
+    def a_block(kz):
+        return w.at[:, at_z(kz), c, top]
+
+    def b_piece(kz):
+        return w.at[y, at_z(kz), c, low]
+
+    def b_block(ky):
+        return w.at[at_y(ky), :, c, low]
+
+    def push(name, ref, device):
+        cp.send(name, ref, ref, device)
+
+    def a_share(kz):
+        push(("as", kz), a_block(kz), other)
+
+    def b_share(ky):
+        push(("bs", ky), b_block(ky), other)
+
+    def a_went(way, k):
+        cp.arrived(("az", way, k), a_block(-way * (k + 1)), to_z[way])
+        if k < (3 if way == 1 else 2):
+            push(("az", way, k + 1), a_block(-way * (k + 1)), to_z[way])
+        a_share(-way * (k + 1))
+
+    def b_went(way, k):
+        cp.arrived(("bz", way, k), b_piece(-way * (k + 1)), to_z[way])
+        if k < (3 if way == -1 else 2):
+            push(("bz", way, k + 1), b_piece(-way * (k + 1)), to_z[way])
+
+    def s0():
+        mine = pltpu.make_async_copy(own, w.at[y, z, c], local_sem)
+        mine.start()
+        for way in (1, -1):
+            cp.send(("ay", way, 0), own.at[top], a_piece(0), to_y[way])
+            cp.send(("bz", way, 0), own.at[low], b_piece(0), to_z[way])
+        mine.wait()
+
+    def s1():
+        cp.arrived(("ay", 1, 0), a_piece(-1), to_y[1])
+        push(("ay", 1, 1), a_piece(-1), to_y[1])
+        b_went(1, 0)
+        b_went(-1, 0)
+
+    def s2():
+        cp.arrived(("ay", -1, 0), a_piece(1), to_y[-1])
+        cp.arrived(("ay", 1, 1), a_piece(-2), to_y[1])
+        for way in (1, -1):
+            push(("az", way, 0), a_block(0), to_z[way])
+        a_share(0)
+        b_went(1, 1)
+        b_went(-1, 1)
+
+    def s3():
+        b_went(1, 2)
+        b_went(-1, 2)
+        a_went(1, 0)
+        a_went(-1, 0)
+
+    def s4():
+        b_went(-1, 3)
+        for way in (1, -1):
+            push(("by", way, 0), b_block(0), to_y[way])
+        b_share(0)
+        a_went(1, 1)
+        a_went(-1, 1)
+
+    def s5():
+        a_went(1, 2)
+        a_went(-1, 2)
+        cp.arrived(("by", -1, 0), b_block(1), to_y[-1])
+        push(("by", -1, 1), b_block(1), to_y[-1])
+        b_share(1)
+        cp.arrived(("by", 1, 0), b_block(-1), to_y[1])
+        b_share(-1)
+
+    def s6():
+        a_went(1, 3)
+        cp.arrived(("by", -1, 1), b_block(2), to_y[-1])
+        b_share(2)
+
+    def s7():
+        for kz in range(-4, 4):
+            where = w.at[:, lax.rem(z - kz * f + 2 * Z, Z), 1 - c, top]
+            cp.arrived(("as", kz), where, other)
+        for ky in range(-1, 3):
+            where = w.at[lax.rem(y - ky * f + 2 * Y, Y), :, 1 - c, low]
+            cp.arrived(("bs", ky), where, other)
+
+    return [s0, s1, s2, s3, s4, s5, s6, s7], [*to_y.values(), *to_z.values(), other]
+
+
+N_WEIGHT_COPIES = 32
+
+
+def greet(devices):
+    barrier = pltpu.get_barrier_semaphore()
+    for device in devices:
+        pl.semaphore_signal(barrier, inc=1, device_id=device, device_id_type=MESH)
+    pl.semaphore_wait(barrier, len(devices))
+
+
+def handoff_body(
+    g_ref, ss_ref, wo_ref, resid_ref, wi_ref, gain_ref, bias_ref, cx_ref, cbc_ref,
+    out_ref, x_ref, bc_ref, step_ref,
+    w_ref, hid_ref, h_ref, opp_ref, right_ref, left_ref, own_ref, sum_r_ref, sum_l_ref,
+    in_l1, in_r1, in_l2, in_r2, ss_in, tail_ref, halo_ref, scale_ref, rs_ref, pre_ref,
+    send_sem, recv_sem, local_sem,
 ):
-    rows, depth = hid_ref.shape
-    width = x_ref.shape[1]
+    rows, width = g_ref.shape
     heads = step_ref.shape[1]
     states = bc_ref.shape[1]
-    first = lax.axis_index("seq") == 0
-
-    def scaled(src, r, at, n, keep):
-        v = src[r, :].astype(F32)
-        rs = lax.rsqrt(jnp.sum(v * v, axis=1, keepdims=True) / depth + 1e-05)
+    seq, me = lax.axis_index("seq"), lax.axis_index("head")
+    n_seq, n_head = lax.axis_size("seq"), lax.axis_size("head")
+    depth = width * n_head
+    r, o, l = (lax.rem(me + k, n_head) for k in (1, 2, 3))
+    right, opposite, left = ((seq, k) for k in (r, o, l))
+    after, before = ((lax.rem(seq + k, n_seq), me) for k in (1, n_seq - 1))
+    cp = Copies(send_sem, recv_sem)
+    steps, partners = weight_steps(cp, wi_ref, w_ref, local_sem)
+    greet([right, left, opposite, after, before, *partners])
+    chunk = rows // NC
+    half = width // 2
+    lo, hi = pl.ds(0, half), pl.ds(half, half)
+    order = [NC - 1 - k for k in range(NC)]
+    tile = 256
+
+    def cut(c):
+        return pl.ds(c * chunk, chunk)
+
+    steps.pop(0)()
+    for k, device in ((1, right), (2, opposite), (3, left)):
+        cp.send(("ss", k), ss_ref, ss_in.at[k - 1], device)
+
+    def product(first, n, dest, store):
+        @pl.loop(0, width // tile)
+        def _(j):
+            at = pl.multiple_of(j * tile, tile)
+            cols = pl.ds(pl.multiple_of(dest * width + at, tile), tile)
+            store(pl.ds(at, tile), bdot(g_ref[pl.ds(first, n), :], wo_ref[:, cols]))
+
+    def project(k):
+        if k % 2:
+            return
+        first, n = order[k + 1] * chunk, 2 * chunk
+        at = pl.ds(first, n)
+
+        def to_opp(cols, p):
+            opp_ref[at, cols] = p.astype(BF16)
+
+        def keep(ref):
+            def store(cols, p):
+                ref[at, cols] = p
+
+            return store
+
+        product(first, n, o, to_opp)
+        for c in (order[k], order[k + 1]):
+            cp.send(("1r", c), opp_ref.at[cut(c), lo], in_l1.at[cut(c)], right)
+            cp.send(("1l", c), opp_ref.at[cut(c), hi], in_r1.at[cut(c)], left)
+        product(first, n, r, keep(right_ref))
+        product(first, n, l, keep(left_ref))
+        product(first, n, me, keep(own_ref))
+
+    def second_sum(c):
+        q = cut(c)
+        cp.arrived(("1r", c), in_l1.at[q], right)
+        sum_r_ref[q, lo] = (right_ref[q, lo] + in_l1[q, :].astype(F32)).astype(BF16)
+        sum_r_ref[q, hi] = right_ref[q, hi].astype(BF16)
+        cp.send(("2r", c), sum_r_ref.at[q], in_l2.at[q], right)
+        cp.arrived(("1l", c), in_r1.at[q], left)
+        sum_l_ref[q, hi] = (left_ref[q, hi] + in_r1[q, :].astype(F32)).astype(BF16)
+        sum_l_ref[q, lo] = left_ref[q, lo].astype(BF16)
+        cp.send(("2l", c), sum_l_ref.at[q], in_r2.at[q], left)
+
+    def token_scale():
+        for k, device in ((1, right), (2, opposite), (3, left)):
+            cp.arrived(("ss", k), ss_in.at[k - 1], device)
+        total = ss_ref[...] + ss_in[0] + ss_in[1] + ss_in[2]
+        eighth = jnp.full((8, 128), 0.125, F32)
+        column = exact_dot(total, eighth, (((0,), (0,)), ((), ())))
+        scale_ref[...] = lax.rsqrt(column / depth + 1e-05)
+
+    def residual(c):
+        q = cut(c)
+        cp.arrived(("2r", c), in_l2.at[q], right)
+        cp.arrived(("2l", c), in_r2.at[q], left)
+        total = own_ref[q, :] + in_l2[q, :].astype(F32) + in_r2[q, :].astype(F32)
+        total = total * scale_ref[q, 0:1] + resid_ref[q, :].astype(F32)
+        out_ref[q, :] = total.astype(BF16)
+        hid_ref[me, q, :] = out_ref[q, :]
+        cp.send(("3r", c), hid_ref.at[me, q], hid_ref.at[me, q], right)
+        cp.send(("3l", c), hid_ref.at[me, q], hid_ref.at[me, q], left)
+
+    def hand_on(c):
+        q = cut(c)
+        cp.arrived(("3r", c), hid_ref.at[l, q], right)
+        cp.send(("4r", c), hid_ref.at[l, q, lo], hid_ref.at[l, q, lo], right)
+        cp.arrived(("3l", c), hid_ref.at[r, q], left)
+        cp.send(("4l", c), hid_ref.at[r, q, hi], hid_ref.at[r, q, hi], left)
+
+    def scaled(src, q, at, n, keep):
+        parts = [src[k, q, :].astype(F32) for k in range(n_head)]
+        total = sum(jnp.sum(v * v, axis=1, keepdims=True) for v in parts)
+        rs = lax.rsqrt(total / depth + 1e-05)
         rs_ref[pl.ds(at, n), :] = jnp.broadcast_to(rs if keep is None else rs * keep, (n, 128))
-        h_ref[pl.ds(at, n), :] = (v * gain_ref[...]).astype(BF16)
-
-    scaled(halo_ref, pl.ds(0, HALO), 0, HALO, jnp.where(first, 0.0, 1.0))
-    step = 64
-
-    @pl.loop(0, rows // step)
-    def _(i):
-        at = pl.multiple_of(i * step, step)
-        scaled(hid_ref, pl.ds(at, step), pl.multiple_of(at + HALO, 16), step, None)
-
-    def project(cols):
-        return bdot(h_ref[...], w_ref[:, cols])
+        for k, v in enumerate(parts):
+            h_ref[k, pl.ds(at, n), :] = (v * gain_ref[:, k * width : (k + 1) * width]).astype(BF16)
+
+    def complete(c):
+        q = cut(c)
+        cp.arrived(("4r", c), hid_ref.at[o, q, lo], right)
+        cp.arrived(("4l", c), hid_ref.at[o, q, hi], left)
+        if c == NC - 1:
+            tail_ref[...] = hid_ref[:, pl.ds(rows - HALO, HALO), :]
+            cp.send("halo", tail_ref, halo_ref, after)
+        scaled(hid_ref, q, c * chunk + HALO, chunk, None)
+
+    for t in range(NC + 4 * CHUNK_LAG):
+        for stage, work in reversed(list(enumerate((project, second_sum, residual, hand_on, complete)))):
+            k = t - CHUNK_LAG * stage
+            if 0 <= k < NC:
+                if work is residual and k == 0:
+                    token_scale()
+                work(k if work is project else order[k])
+        if steps:
+            steps.pop(0)()
+    while steps:
+        steps.pop(0)()
+    cp.arrived("halo", halo_ref, after)
+    scaled(halo_ref, pl.ds(0, HALO), 0, HALO, jnp.where(seq == 0, 0.0, 1.0))
+
+    def into(cols, at, n):
+        total = None
+        for k in range(n_head):
+            piece = bdot(
+                h_ref[k, pl.ds(at, n), :], w_ref[k, :, :, :, cols].reshape(width, cols.size)
+            )
+            total = piece if total is None else total + piece
+        return total
 
     def conv(taps, k):
         n = taps.shape[1]
@@ -220,22 +495,60 @@
             total = v if total is None else total + v
         return (total / (1.0 + jnp.exp(-total))).astype(BF16)
 
-    tile = 256
-    rs_all = rs_ref[...]
-    rs2 = jnp.concatenate([rs_all, rs_all], axis=1)
+    every = rows + HALO
+
+    def pre(cols):
+        rs = rs_ref[...]
+        pre_ref[...] = (into(cols, 0, every) * jnp.concatenate([rs, rs], axis=1)).astype(BF16).astype(F32)
 
     @pl.loop(0, width // tile)
     def _(i):
-        at = pl.multiple_of(i * tile, tile)
-        cols = pl.ds(at, tile)
-        pre_ref[...] = (project(cols) * rs2).astype(BF16).astype(F32)
+        cols = pl.ds(pl.multiple_of(i * tile, tile), tile)
+        pre(cols)
         x_ref[:, cols] = conv(cx_ref[:, cols], cx_ref.shape[0])
 
-    pre_ref[...] = (project(pl.ds(width, states)) * rs2).astype(BF16).astype(F32)
+    pre(pl.ds(width, states))
     bc_ref[...] = conv(cbc_ref[...], cbc_ref.shape[0])
-    dt = bdot(h_ref[pl.ds(HALO, rows), :], w_ref[:, pl.ds(width + states, 128)])
+    dt = into(pl.ds(width + states, 128), HALO, rows)
     dt = (dt * rs_ref[pl.ds(HALO, rows), :])[:, :heads] + bias_ref[...]
     step_ref[...] = jnp.maximum(dt, 0.0) + jnp.log(1.0 + jnp.exp(-jnp.abs(dt)))
+    cp.finish()
+
+
+def handoff(g, ss, w_out_all, resid, w_in, gain, bias, conv_x, conv_bc, heads):
+    rows, width = g.shape
+    n_head = lax.axis_size("head")
+    states = conv_bc.shape[1]
+    copies = N_WEIGHT_COPIES + 3 + 1 + 8 * NC
+    return call(
+        handoff_body,
+        (
+            sds(rows, width, dtype=BF16), sds(rows, width, dtype=BF16),
+            sds(rows, states, dtype=BF16), sds(rows, heads),
+        ),
+        (g, ss, w_out_all, resid, w_in, gain, bias, conv_x, conv_bc),
+        [
+            pltpu.VMEM((Y, Z, CORES, *w_in.shape), BF16),
+            pltpu.VMEM((n_head, rows, width), BF16),
+            pltpu.VMEM((n_head, rows + HALO, width), BF16),
+            pltpu.VMEM((rows, width), BF16),
+            *[pltpu.VMEM((rows, width), F32) for _ in range(3)],
+            *[pltpu.VMEM((rows, width), BF16) for _ in range(2)],
+            *[pltpu.VMEM((rows, width // 2), BF16) for _ in range(2)],
+            *[pltpu.VMEM((rows, width), BF16) for _ in range(2)],
+            pltpu.VMEM((3, *ss.shape), F32),
+            *[pltpu.VMEM((n_head, HALO, width), BF16) for _ in range(2)],
+            pltpu.VMEM((rows, 128), F32),
+            pltpu.VMEM((rows + HALO, 128), F32),
+            pltpu.VMEM((rows + HALO, 256), F32),
+            pltpu.SemaphoreType.DMA((copies,)),
+            pltpu.SemaphoreType.DMA((copies,)),
+            pltpu.SemaphoreType.DMA,
+        ],
+        limit=60,
+        collective_id=1,
+        has_side_effects=True,
+    )
 
 
 def call(body, outs, args, scratch=(), limit=56, **kw):
@@ -292,7 +605,6 @@
     w_in = jnp.concatenate(
         [w_in_x, w_in_bc, jnp.pad(w_in_dt, ((0, 0), (0, 128 - heads)))], axis=1
     )
-    w_in_all = lax.all_gather(w_in, "seq", axis=0, tiled=True)
 
     send, st, cum = local_states(x_in, bc_in, step_in, decay_code[0], decay_rate[0:1])
     y = diagonal(x_in, bc_in, step_in, cum, skip_gain[0:1])
@@ -302,23 +614,8 @@
         (sds(rows, width, dtype=BF16), sds(8, rows)),
         (bc_in, cum, prev, st, y, gate_in, norm_gain[None, :]),
     )
-    rs = lax.rsqrt(lax.psum(ss[0], "head") / inner + 1e-05)
-    projected = jnp.dot(g, w_out_all, preferred_element_type=F32).astype(BF16)
-    share = lax.psum_scatter(projected, "head", scatter_dimension=1, tiled=True)
-    resid_out = (resid_in.astype(F32) + share.astype(F32) * rs[:, None]).astype(BF16)
-    hidden = lax.all_gather(resid_out, "head", axis=1, tiled=True)
-    size = lax.axis_size("seq")
-    halo = lax.ppermute(hidden[rows - HALO :], "seq", [(i, i + 1) for i in range(size - 1)])
-
-    x_two, bc_two, step_two = call(
-        second_body,
-        (sds(rows, width, dtype=BF16), sds(*bc_in.shape, dtype=BF16), sds(rows, heads)),
-        (hidden, halo, resid_gain[None, :], w_in_all, step_time_bias[None, :], conv_x, conv_bc),
-        [
-            pltpu.VMEM((rows + HALO, inner), BF16),
-            pltpu.VMEM((rows + HALO, 256), F32),
-            pltpu.VMEM((rows + HALO, 128), F32),
-        ],
+    resid_out, x_two, bc_two, step_two = handoff(
+        g, ss, w_out_all, resid_in, w_in, resid_gain[None, :], step_time_bias[None, :], conv_x, conv_bc, heads
     )
     send, st, cum = local_states(x_two, bc_two, step_two, decay_code[1], decay_rate[1:2])
     y = diagonal(x_two, bc_two, step_two, cum, skip_gain[1:2])

time: 396 us -> 306 us (0.77)
  waiting for transfers between devices: 206 us -> 31.2 us
  Pallas kernels: 56.2 us -> 153 us
  local copies, waits for them, and re-layouts: 16.4 us -> 26.6 us
  matrix products: 10.2 us -> 0 us
  blocking collectives: 62.5 us -> 56.9 us
  starting transfers between devices: 16.7 us -> 12.3 us
    all_gather x2 -> x0, waiting for transfers between devices: 136 us -> none  [the longest x1 86.6 us: on_device(): w_in_all = lax.all_gather(w_in, 'seq', axis=0, tiled=True)]
    pallas_call x9, Pallas kernels: 56.2 us -> 153 us  [call(): pl.pallas_call(body, out_shape=outs, in_specs=[VMEM] * len(args), out_spe...]
    reduce_scatter x1 -> x0, waiting for transfers between devices: 37.4 us -> none  [on_device(): share = lax.psum_scatter(projected, 'head', scatter_dimension=1, tiled=True)]
    all_gather x0 -> x1, local copies, waits for them, and re-layouts: none -> 11.5 us  [on_device(): w_out_all = lax.all_gather(w_out, 'seq', axis=1, tiled=True)]
    dot_general x1 -> x0, matrix products: 10.2 us -> none  [on_device(): projected = jnp.dot(g, w_out_all, preferred_element_type=F32).astype(BF16)]
    psum x2 -> x1, blocking collectives: 17.3 us -> 9.21 us  [on_device(): rs = lax.rsqrt(lax.psum(ss[0], 'head') / inner + 1e-05)]
    ppermute x1 -> x0, starting transfers between devices: 4 us -> none  [on_device(): lax.ppermute(hidden[rows - HALO:], 'seq', [(i, i + 1) for i in range(size...]
    unnamed x28 -> x27, local copies, waits for them, and re-layouts: 10.7 us -> 11 us
  transfers between devices with their start and end apart: 7 -> 3, of which waited for: 6 -> 3; matrix products, arithmetic and copies ran while one was open for 4% -> 5% of each run, Pallas kernels for 6% -> 8%
where the time goes in v1:
time: 306 us; the launch traced here: 304 us
  Pallas kernels  153 us (50%)
  blocking collectives  56.9 us (19%)
  waiting for transfers between devices  31.2 us (10%)
  local copies, waits for them, and re-layouts  26.6 us (9%)
  between operations  14.2 us (5%)
  starting transfers between devices  12.3 us (4%)
  other arithmetic  10.2 us (3%)
    pallas_call x9, Pallas kernels, call(): pl.pallas_call(body, out_shape=outs, in_specs=[VMEM] * len(args), out_spe...  153 us
    all_to_all x2, blocking collectives, prefix(): got = lax.all_to_all(send, 'seq', 0, 0, tiled=True)  47.7 us
    all_gather x1, waiting for transfers between devices, on_device(): w_out_all = lax.all_gather(w_out, 'seq', axis=1, tiled=True)  20.3 us
    all_to_all x2, starting transfers between devices, prefix(): return lax.all_to_all(back, 'seq', 0, 0, tiled=True)  12.2 us
    all_gather x1, local copies, waits for them, and re-layouts, on_device(): w_out_all = lax.all_gather(w_out, 'seq', axis=1, tiled=True)  11.5 us
    unnamed x27, local copies, waits for them, and re-layouts  11 us
    all_to_all x2, waiting for transfers between devices, prefix(): return lax.all_to_all(back, 'seq', 0, 0, tiled=True)  10.2 us
    psum x1, blocking collectives, on_device(): rs = lax.rsqrt(lax.psum(ss[0], 'head') / inner + 1e-05)  9.21 us
  transfers between devices with their start and end apart: 3, of which 3 were waited for; matrix products, arithmetic and copies ran while one was open for 5% of the time, Pallas kernels for 8%

profile of v1, /device:TPU:1, one launch (start us, length us, event | category | flops | bytes accessed | tf_op | source)
XLA Modules:
  0.0 304.4 jit_solution(9919762206588849103)
XLA Ops:
  7.2 0.0 all-gather.2.cloned.1.call-start
  7.2 0.7 all-gather.2.cloned.1.call-update
  7.9 1.6 copy.36.step_ref
  9.5 0.8 fusion.2
  10.3 0.9 copy.49
  11.1 1.4 fusion.4
  12.5 4.7 %shard_map.176 = (bf16[64,2176]{1,0:T(8,128)(2,1)}, f32[128,1024]{1,0:T(8,128)}, f32[512,16]{1,0:T(8,128)}) custom-call(bf16[512,1024]{1,0:T(8,128)(2,1)} %x_ref.3, bf16[512,256]{1,0:T(8,128)(2,1)} %bc_ref.5, f32[512,16]{1,0:T(8,128)} %copy.36.step_ref, s32[512,16]{1,0:T(8,128)} %bitcast.28, f32[1,16]{1,0:T(1,128)} %get-tuple-element.35.rate_ref), custom_call_target="tpu_custom_call" | custom-call | tf_op jit(solution)/shard_map/pallas_call | solution.py:555
  17.2 0.6 broadcast.8
  17.7 1.7 reduce
  19.4 0.3 reshape.13
  19.7 0.0 copy-start.3
  19.7 27.0 %all_to_all.44 = bf16[64,2,1088]{2,1,0:T(2,128)(2,1)S(1)} all-to-all(bf16[64,2,1088]{2,1,0:T(2,128)(2,1)S(1)} %reshape.13), channel_id=1, replica_groups=mesh['seq'=64,'head'=4] {'seq'}, dimensions={0} | all-to-all | bytes 557056 | tf_op jit(solution)/shard_map/all_to_all | solution.py:571
  46.8 0.0 copy-start.4
  46.8 0.3 reshape.14
  47.1 0.7 copy.56
  47.9 2.6 shard_map.177
  50.5 1.7 reduce.1
  52.2 0.9 reshape.15
  53.0 6.1 %all-to-all-start.1 = ((bf16[64,2,1024]{2,1,0:T(2,128)(2,1)}), bf16[64,2,1024]{2,1,0:T(2,128)(2,1)S(1)}, u32[]{:S(2)}, u32[]{:S(2)}) async-start(bf16[64,2,1024]{2,1,0:T(2,128)(2,1)} %reshape.15), calls=%async_computation.1 | async-start | bytes 524288 | tf_op jit(solution)/shard_map/all_to_all | solution.py:579
  59.2 0.0 copy-done.3
  59.2 0.1 copy.40
  59.3 0.0 copy-start.1
  59.3 0.0 copy-start.2
  59.3 0.8 copy.50
  60.2 0.0 copy-done.4
  60.2 0.6 fusion.3
  60.7 5.8 %shard_map.178.y_ref = f32[512,1024]{1,0:T(8,128)} custom-call(bf16[512,1024]{1,0:T(8,128)(2,1)} %x_ref.3, bf16[512,256]{1,0:T(8,128)(2,1)} %bc_ref.5, f32[512,16]{1,0:T(8,128)} %copy.36.step_ref, f32[512,16]{1,0:T(8,128)} %get-tuple-element.16.cum_ref, f32[1,16]{1,0:T(1,128)} %get-tuple-element.33.skip_ref), custom_call_target="tpu_custom_call" | custom-call | tf_op jit(solution)/shard_map/pallas_call | solution.py:555
  66.5 0.0 copy-done.1
  66.5 0.0 copy-done.2
  66.5 0.7 fusion.1.wi_ref
  67.2 4.0 %all-to-all-done.1 = bf16[64,2,1024]{2,1,0:T(2,128)(2,1)S(1)} async-done(((bf16[64,2,1024]{2,1,0:T(2,128)(2,1)}), bf16[64,2,1024]{2,1,0:T(2,128)(2,1)S(1)}, u32[]{:S(2)}, u32[]{:S(2)}) %all-to-all-start.1) | async-done | bytes 262176 | tf_op jit(solution)/shard_map/all_to_all | solution.py:579
  71.2 0.2 reshape.16
  71.4 0.9 copy.58
  72.3 6.6 %shard_map.179 = (bf16[512,1024]{1,0:T(8,128)(2,1)}, f32[8,512]{1,0:T(8,128)}) custom-call(bf16[512,256]{1,0:T(8,128)(2,1)} %bc_ref.5, f32[512,16]{1,0:T(8,128)} %get-tuple-element.16.cum_ref, bf16[64,2048]{1,0:T(8,128)(2,1)} %bitcast.24, f32[128,1024]{1,0:T(8,128)} %get-tuple-element.18.st_ref, f32[512,1024]{1,0:T(8,128)} %shard_map.178.y_ref, ...), custom_call_target="tpu_custom_call" | custom-call | tf_op jit(solution)/shard_map/pallas_call | solution.py:555
  78.9 20.3 %all-gather.2.cloned.1.call-done = bf16[1024,4096]{0,1:T(8,128)(2,1)} async-done(((bf16[1024,64]{0,1:T(8,128)(2,1)}), bf16[1024,4096]{0,1:T(8,128)(2,1)}) %all-gather.2.cloned.1.call-update) | async-done | bytes 8388624 | tf_op jit(solution)/shard_map/all_gather | solution.py:604
  99.2 11.5 %copy.41.wo_ref = bf16[1024,4096]{1,0:T(8,128)(2,1)} copy(bf16[1024,4096]{0,1:T(8,128)(2,1)} %all-gather.2.cloned.1.call-done) | data formatting | bytes 16777216 | tf_op jit(solution)/shard_map/all_gather | solution.py:604
  110.7 114.7 %shard_map.180 = (bf16[512,1024]{1,0:T(8,128)(2,1)}, bf16[512,1024]{1,0:T(8,128)(2,1)}, bf16[512,256]{1,0:T(8,128)(2,1)}, f32[512,16]{1,0:T(8,128)}) custom-call(bf16[512,1024]{1,0:T(8,128)(2,1)} %get-tuple-element.19.g_ref, f32[8,512]{1,0:T(8,128)} %get-tuple-element.20.ss_ref, bf16[1024,4096]{1,0:T(8,128)(2,1)} %copy.41.wo_ref, ...), custom_call_target="tpu_custom_call" | custom-call | tf_op jit(solution)/shard_map/pallas_call | solution.py:555
  225.4 4.7 %shard_map.181 = (bf16[64,2176]{1,0:T(8,128)(2,1)}, f32[128,1024]{1,0:T(8,128)}, f32[512,16]{1,0:T(8,128)}) custom-call(bf16[512,1024]{1,0:T(8,128)(2,1)} %get-tuple-element.23.x_ref, bf16[512,256]{1,0:T(8,128)(2,1)} %get-tuple-element.22.bc_ref, f32[512,16]{1,0:T(8,128)} %get-tuple-element.24.step_ref, s32[512,16]{1,0:T(8,128)} %bitcast.27, ...), custom_call_target="tpu_custom_call" | custom-call | tf_op jit(solution)/shard_map/pallas_call | solution.py:555
  230.1 1.7 reduce.2
  231.8 0.3 reshape.17
  232.1 20.7 %all_to_all.45 = bf16[64,2,1088]{2,1,0:T(2,128)(2,1)S(1)} all-to-all(bf16[64,2,1088]{2,1,0:T(2,128)(2,1)S(1)} %reshape.17), channel_id=1, replica_groups=mesh['seq'=64,'head'=4] {'seq'}, dimensions={0} | all-to-all | bytes 557056 | tf_op jit(solution)/shard_map/all_to_all | solution.py:571
  252.8 0.3 reshape.18
  253.1 0.7 copy.55
  253.9 2.5 shard_map.182
  256.4 1.7 reduce.3
  258.1 0.9 reshape.19
  259.0 6.1 %all-to-all-start.3 = ((bf16[64,2,1024]{2,1,0:T(2,128)(2,1)}), bf16[64,2,1024]{2,1,0:T(2,128)(2,1)S(1)}, u32[]{:S(2)}, u32[]{:S(2)}) async-start(bf16[64,2,1024]{2,1,0:T(2,128)(2,1)} %reshape.19), calls=%async_computation.3 | async-start | bytes 524288 | tf_op jit(solution)/shard_map/all_to_all | solution.py:579
  265.1 5.8 %shard_map.183.y_ref = f32[512,1024]{1,0:T(8,128)} custom-call(bf16[512,1024]{1,0:T(8,128)(2,1)} %get-tuple-element.23.x_ref, bf16[512,256]{1,0:T(8,128)(2,1)} %get-tuple-element.22.bc_ref, f32[512,16]{1,0:T(8,128)} %get-tuple-element.24.step_ref, f32[512,16]{1,0:T(8,128)} %get-tuple-element.25.cum_ref, f32[1,16]{1,0:T(1,128)} %get-tuple-element.32.skip_ref), custom_call_target="tpu_custom_call" | custom-call | tf_op jit(solution)/shard_map/pallas_call | solution.py:555
  270.8 6.2 %all-to-all-done.3 = bf16[64,2,1024]{2,1,0:T(2,128)(2,1)S(1)} async-done(((bf16[64,2,1024]{2,1,0:T(2,128)(2,1)}), bf16[64,2,1024]{2,1,0:T(2,128)(2,1)S(1)}, u32[]{:S(2)}, u32[]{:S(2)}) %all-to-all-start.3) | async-done | bytes 262176 | tf_op jit(solution)/shard_map/all_to_all | solution.py:579
  277.1 0.2 reshape.20
  277.3 0.9 copy.57
  278.1 5.6 %shard_map.184 = (f32[512,1024]{1,0:T(8,128)}, f32[8,512]{1,0:T(8,128)}) custom-call(bf16[512,256]{1,0:T(8,128)(2,1)} %get-tuple-element.22.bc_ref, f32[512,16]{1,0:T(8,128)} %get-tuple-element.25.cum_ref, bf16[64,2048]{1,0:T(8,128)(2,1)} %bitcast.29, f32[128,1024]{1,0:T(8,128)} %get-tuple-element.27.st_ref, f32[512,1024]{1,0:T(8,128)} %shard_map.183.y_ref), custom_call_target="tpu_custom_call" | custom-call | tf_op jit(solution)/shard_map/pallas_call | solution.py:555
  283.8 0.0 copy-start
  283.8 0.8 slice.27
  284.6 9.2 %psum.7 = f32[512]{0:T(512)S(1)} all-reduce(f32[512]{0:T(512)S(1)} %bitcast.33), channel_id=1, replica_groups=mesh['seq'=64,'head'=4] {'head'}, use_global_device_ids=true, to_apply=%region_0.1 | all-reduce | flops 512 | bytes 4096 | tf_op jit(solution)/shard_map/psum | solution.py:624
  293.8 2.7 multiply_convert_fusion
  296.5 0.0 copy-done
  296.6 1.0 copy.64
  (1 shorter events, 0.0 us)
Async XLA Ops:
  7.2 92.0 %all-gather.2.cloned.1.call-start = ((), (), s32[]{:S(2)}) async-start(), calls=%async_computation.4 | async-start | bytes 8519680 | tf_op jit(solution)/shard_map/all_gather | solution.py:604
  19.7 39.5 %copy-start.3 = (bf16[64,16]{0,1:T(8,128)(2,1)S(1)}, bf16[64,16]{0,1:T(8,128)(2,1)}, u32[]{:S(2)}) copy-start(bf16[64,16]{0,1:T(8,128)(2,1)} %param.30) | copy-start | bytes 6148
  46.8 13.4 %copy-start.4 = (f32[2,16]{1,0:T(2,128)S(1)}, f32[2,16]{1,0:T(2,128)}, u32[]{:S(2)}) copy-start(f32[2,16]{1,0:T(2,128)} %param.23) | copy-start | bytes 388
  53.0 18.1 %all-to-all-start.1 = ((bf16[64,2,1024]{2,1,0:T(2,128)(2,1)}), bf16[64,2,1024]{2,1,0:T(2,128)(2,1)S(1)}, u32[]{:S(2)}, u32[]{:S(2)}) async-start(bf16[64,2,1024]{2,1,0:T(2,128)(2,1)} %reshape.15), calls=%async_computation.1 | async-start | bytes 524288 | tf_op jit(solution)/shard_map/all_to_all | solution.py:579
  59.3 7.2 %copy-start.1 = (bf16[64,1024]{1,0:T(8,128)(2,1)S(1)}, bf16[64,1024]{1,0:T(8,128)(2,1)}, u32[]{:S(2)}) copy-start(bf16[64,1024]{1,0:T(8,128)(2,1)} %param.28) | copy-start | bytes 393220
  59.3 7.2 %copy-start.2 = (bf16[64,256]{1,0:T(8,128)(2,1)S(1)}, bf16[64,256]{1,0:T(8,128)(2,1)}, u32[]{:S(2)}) copy-start(bf16[64,256]{1,0:T(8,128)(2,1)} %param.29) | copy-start | bytes 98308
  259.0 18.1 %all-to-all-start.3 = ((bf16[64,2,1024]{2,1,0:T(2,128)(2,1)}), bf16[64,2,1024]{2,1,0:T(2,128)(2,1)S(1)}, u32[]{:S(2)}, u32[]{:S(2)}) async-start(bf16[64,2,1024]{2,1,0:T(2,128)(2,1)} %reshape.19), calls=%async_computation.3 | async-start | bytes 524288 | tf_op jit(solution)/shard_map/all_to_all | solution.py:579
  283.8 12.8 %copy-start = (bf16[512,1024]{1,0:T(8,128)(2,1)S(1)}, bf16[512,1024]{1,0:T(8,128)(2,1)}, u32[]{:S(2)}) copy-start(bf16[512,1024]{1,0:T(8,128)(2,1)} %get-tuple-element.38) | copy-start | bytes 3145732
Sparse Core Ops, SparseCore 0:
  10.8 88.3 all-gather.1

commit v2 on v1

--- a/solution.py
+++ b/solution.py
@@ -1,4 +1,5 @@
 import functools
+import types
 
 import jax
 import jax.numpy as jnp
@@ -48,15 +49,13 @@
     return iota((n, n), 0) >= iota((n, n), 1)
 
 
-def states_body(x_ref, bc_ref, step_ref, code_ref, rate_ref, send_ref, st_ref, cum_ref):
+def states_body(x_ref, bc_ref, step_ref, code_ref, rate, st_ref, end_ref, total_ref, cum_ref):
     rows, heads = step_ref.shape
-    blocks = rows // GROUP
     tri = lower(GROUP).astype(F32)
-    totals = []
-    state = None
-    for b in range(blocks):
+    total = state = None
+    for b in range(rows // GROUP):
         r = pl.ds(b * GROUP, GROUP)
-        decay = -jnp.minimum(code_ref[r, :].astype(F32) * rate_ref[...], 20.0)
+        decay = -jnp.minimum(code_ref[r, :].astype(F32) * rate, 20.0)
         cum = exact_dot(tri, decay)
         cum_ref[r, :] = cum
         last = cum[GROUP - 1 : GROUP, :]
@@ -66,63 +65,33 @@
             bc_ref[r, : bc_ref.shape[1] // 2], v, (((0,), (0,)), ((), ())), preferred_element_type=F32
         )
         if state is None:
-            state = term
             st_ref[...] = term
+            state, total = term, last
         else:
             factor = spread(jnp.broadcast_to(jnp.exp(last), (8, heads)), heads)[0:1]
-            state = factor * state + term
-        totals.append(last)
-    half = state.shape[0] // 2
-    width = state.shape[1]
-    send_ref[:, :width] = state[:half].astype(BF16)
-    send_ref[:, width : 2 * width] = state[half:].astype(BF16)
-    total = sum(totals[1:], totals[0])
-    pieces = []
-    rest = total
-    for _ in range(3):
-        piece = rest.astype(BF16).astype(F32)
-        pieces.append(piece)
-        rest = rest - piece
-    pieces.append(jnp.zeros((1, 128 - 3 * heads), F32))
-    tail = jnp.concatenate(pieces, axis=1)
-    send_ref[:, 2 * width :] = jnp.broadcast_to(tail, (half, 128)).astype(BF16)
-
-
-def scan_body(heads, got_ref, out_ref, s_ref, d_ref, p_ref):
-    count = got_ref.shape[0]
-    width = heads * CH
-    s_ref[...] = got_ref[:, : 2 * width].astype(F32)
-    tail = got_ref[:, 2 * width :].astype(F32)
-    total = tail[:, :heads] + tail[:, heads : 2 * heads] + tail[:, 2 * heads : 3 * heads]
-    d = spread(jnp.exp(total), heads)
-    d_ref[:, :width] = d
-    d_ref[:, width:] = d
-
-    def one(k, p):
-        row = pl.ds(k, 1)
-        p_ref[row, :] = p
-        return d_ref[row, :] * p + s_ref[row, :]
-
-    lax.fori_loop(0, count, one, jnp.zeros((1, 2 * width), F32))
-    out_ref[...] = p_ref[...].astype(BF16)
-
-
-def diag_body(x_ref, bc_ref, step_ref, cum_ref, skip_ref, y_ref):
+            state, total = factor * state + term, total + last
+    end_ref[...] = state
+    wide = jnp.concatenate([total, jnp.zeros((1, 128 - heads), F32)], axis=1)
+    total_ref[...] = jnp.broadcast_to(wide, (8, 128))
+
+
+def diag_pieces(x_ref, bc_ref, step_ref, cum_ref, skip, y_ref):
     rows, heads = step_ref.shape
     n = bc_ref.shape[1] // 2
     half = GROUP // 2
-    eye = (iota((heads, heads), 0) == iota((heads, heads), 1)).astype(F32)
-    left = iota((GROUP, 2 * CH), 1) < CH
-    skip = spread(jnp.broadcast_to(skip_ref[...], (8, heads)), heads)[0:1]
     zero = jnp.zeros((), BF16)
-    for b in range(rows // GROUP):
+
+    def piece(b, pairs):
         r = pl.ds(b * GROUP, GROUP)
+        eye = (iota((heads, heads), 0) == iota((heads, heads), 1)).astype(F32)
+        left = iota((GROUP, 2 * CH), 1) < CH
+        gains = spread(jnp.broadcast_to(skip, (8, heads)), heads)[0:1]
         scores = bdot(bc_ref[r, n:], bc_ref[r, :n], NT)
         scores = jnp.where(lower(GROUP), scores, 0.0)
         cum = cum_ref[r, :]
         cum_row = exact_dot(eye, cum, NT)
         step_row = exact_dot(eye, step_ref[r, :], NT)
-        for pair in range(heads // 2):
+        for pair in pairs:
             lanes = pl.ds(pair * 2 * CH, 2 * CH)
             xp = x_ref[r, lanes]
             tops, bottoms = [], []
@@ -142,23 +111,29 @@
                 ).astype(BF16)
                 tops.append(bdot(top, mine[:half]))
                 bottoms.append(bdot(bottom, mine))
-            xs = xp.astype(F32) * skip[:, pair * 2 * CH : (pair + 1) * 2 * CH]
+            xs = xp.astype(F32) * gains[:, pair * 2 * CH : (pair + 1) * 2 * CH]
             y_ref[pl.ds(b * GROUP, half), lanes] = tops[0] + tops[1] + xs[:half]
             y_ref[pl.ds(b * GROUP + half, half), lanes] = bottoms[0] + bottoms[1] + xs[half:]
 
+    quarter = heads // 4
+    return [
+        functools.partial(piece, b, range(k * quarter, (k + 1) * quarter))
+        for b in range(rows // GROUP)
+        for k in range(2)
+    ]
+
 
 def mixed_blocks(bc_ref, cum_ref, prev_ref, st_ref, y_ref):
     rows, heads = cum_ref.shape
-    width = heads * CH
     n = bc_ref.shape[1] // 2
     out = []
-    low = high = None
+    high = None
     for b in range(rows // GROUP):
         r = pl.ds(b * GROUP, GROUP)
         c = bc_ref[r, n:]
         cum = cum_ref[r, :]
         if b == 0:
-            high = jnp.concatenate([prev_ref[:, :width], prev_ref[:, width:]], axis=0)
+            high = prev_ref[...]
             inner = bdot(c, high)
         else:
             last = cum_ref[pl.ds(GROUP - 8, 8), :]
@@ -170,12 +145,12 @@
     return out
 
 
-def gate_body(bc_ref, cum_ref, prev_ref, st_ref, y_ref, gate_ref, gain_ref, g_ref, ss_ref):
+def gate_body(bc_ref, cum_ref, prev_ref, st_ref, y_ref, gate_ref, gain, g_ref, ss_ref):
     ones = jnp.ones((8, g_ref.shape[1]), F32)
     for r, mixed in mixed_blocks(bc_ref, cum_ref, prev_ref, st_ref, y_ref):
         gate = gate_ref[r, :].astype(F32)
         gated = mixed * (gate / (1.0 + jnp.exp(-gate)))
-        g_ref[r, :] = (gated * gain_ref[...]).astype(BF16)
+        g_ref[r, :] = (gated * gain).astype(BF16)
         ss_ref[:, r] = exact_dot(ones, gated * gated, NT)
 
 
@@ -227,7 +202,7 @@
             copy.wait_send()
 
 
-def weight_steps(cp, own, w, local_sem):
+def weight_steps(cp, tag, own, w, local_sem):
     y, z, c = place()
     head = lax.axis_index("head")
     half = own.shape[0] // 2
@@ -260,41 +235,41 @@
         cp.send(name, ref, ref, device)
 
     def a_share(kz):
-        push(("as", kz), a_block(kz), other)
+        push((tag, "as", kz), a_block(kz), other)
 
     def b_share(ky):
-        push(("bs", ky), b_block(ky), other)
+        push((tag, "bs", ky), b_block(ky), other)
 
     def a_went(way, k):
-        cp.arrived(("az", way, k), a_block(-way * (k + 1)), to_z[way])
+        cp.arrived((tag, "az", way, k), a_block(-way * (k + 1)), to_z[way])
         if k < (3 if way == 1 else 2):
-            push(("az", way, k + 1), a_block(-way * (k + 1)), to_z[way])
+            push((tag, "az", way, k + 1), a_block(-way * (k + 1)), to_z[way])
         a_share(-way * (k + 1))
 
     def b_went(way, k):
-        cp.arrived(("bz", way, k), b_piece(-way * (k + 1)), to_z[way])
+        cp.arrived((tag, "bz", way, k), b_piece(-way * (k + 1)), to_z[way])
         if k < (3 if way == -1 else 2):
-            push(("bz", way, k + 1), b_piece(-way * (k + 1)), to_z[way])
+            push((tag, "bz", way, k + 1), b_piece(-way * (k + 1)), to_z[way])
 
     def s0():
         mine = pltpu.make_async_copy(own, w.at[y, z, c], local_sem)
         mine.start()
         for way in (1, -1):
-            cp.send(("ay", way, 0), own.at[top], a_piece(0), to_y[way])
-            cp.send(("bz", way, 0), own.at[low], b_piece(0), to_z[way])
+            cp.send((tag, "ay", way, 0), own.at[top], a_piece(0), to_y[way])
+            cp.send((tag, "bz", way, 0), own.at[low], b_piece(0), to_z[way])
         mine.wait()
 
     def s1():
-        cp.arrived(("ay", 1, 0), a_piece(-1), to_y[1])
-        push(("ay", 1, 1), a_piece(-1), to_y[1])
+        cp.arrived((tag, "ay", 1, 0), a_piece(-1), to_y[1])
+        push((tag, "ay", 1, 1), a_piece(-1), to_y[1])
         b_went(1, 0)
         b_went(-1, 0)
 
     def s2():
-        cp.arrived(("ay", -1, 0), a_piece(1), to_y[-1])
-        cp.arrived(("ay", 1, 1), a_piece(-2), to_y[1])
+        cp.arrived((tag, "ay", -1, 0), a_piece(1), to_y[-1])
+        cp.arrived((tag, "ay", 1, 1), a_piece(-2), to_y[1])
         for way in (1, -1):
-            push(("az", way, 0), a_block(0), to_z[way])
+            push((tag, "az", way, 0), a_block(0), to_z[way])
         a_share(0)
         b_went(1, 1)
         b_went(-1, 1)
@@ -308,7 +283,7 @@
     def s4():
         b_went(-1, 3)
         for way in (1, -1):
-            push(("by", way, 0), b_block(0), to_y[way])
+            push((tag, "by", way, 0), b_block(0), to_y[way])
         b_share(0)
         a_went(1, 1)
         a_went(-1, 1)
@@ -316,26 +291,131 @@
     def s5():
         a_went(1, 2)
         a_went(-1, 2)
-        cp.arrived(("by", -1, 0), b_block(1), to_y[-1])
-        push(("by", -1, 1), b_block(1), to_y[-1])
+        cp.arrived((tag, "by", -1, 0), b_block(1), to_y[-1])
+        push((tag, "by", -1, 1), b_block(1), to_y[-1])
         b_share(1)
-        cp.arrived(("by", 1, 0), b_block(-1), to_y[1])
+        cp.arrived((tag, "by", 1, 0), b_block(-1), to_y[1])
         b_share(-1)
 
     def s6():
         a_went(1, 3)
-        cp.arrived(("by", -1, 1), b_block(2), to_y[-1])
+        cp.arrived((tag, "by", -1, 1), b_block(2), to_y[-1])
         b_share(2)
 
     def s7():
         for kz in range(-4, 4):
             where = w.at[:, lax.rem(z - kz * f + 2 * Z, Z), 1 - c, top]
-            cp.arrived(("as", kz), where, other)
+            cp.arrived((tag, "as", kz), where, other)
         for ky in range(-1, 3):
             where = w.at[lax.rem(y - ky * f + 2 * Y, Y), :, 1 - c, low]
-            cp.arrived(("bs", ky), where, other)
+            cp.arrived((tag, "bs", ky), where, other)
 
     return [s0, s1, s2, s3, s4, s5, s6, s7], [*to_y.values(), *to_z.values(), other]
+
+
+def prefix_steps(cp, tag, heads, end_ref, total_ref, prev_ref, p):
+    y, z, c = place()
+    head = lax.axis_index("head")
+    other = (seq_of(y, z, 1 - c), head)
+    n, width = end_ref.shape
+    half, lanes, part = n // 2, width // 2, heads // 2
+    to_z = {k: (seq_of(y, lax.rem(z + k, Z), c), head) for k in range(1, Z)}
+    to_y = {k: (seq_of(lax.rem(y + k, Y), z, c), head) for k in range(1, Y)}
+    mine = pl.ds(pl.multiple_of(c * half, half), half)
+    theirs = pl.ds(pl.multiple_of((1 - c) * half, half), half)
+    first = c == 0
+
+    def cell(j):
+        return pl.ds((j // 2) * 16, 16), pl.ds((j % 2) * lanes, lanes)
+
+    def factor(log):
+        return spread(jnp.exp(log), part)
+
+    def log_of(tail):
+        return tail[:, :part] + tail[:, part : 2 * part] + tail[:, 2 * part : 3 * part]
+
+    def core_out():
+        p.pair_out[pl.ds(0, half), :] = end_ref[theirs, :]
+        p.pair_out[pl.ds(half, 8), pl.ds(0, 128)] = total_ref[...]
+        p.pair_out[pl.ds(half, 8), pl.ds(128, width - 128)] = jnp.zeros((8, width - 128), F32)
+        cp.send((tag, "out"), p.pair_out, p.pair_in, other)
+
+    def z_out():
+        cp.arrived((tag, "out"), p.pair_in, other)
+        own, got = end_ref[mine, :], p.pair_in[pl.ds(0, half), :]
+        own_log = total_ref[:, :heads]
+        got_log = p.pair_in[pl.ds(half, 8), pl.ds(0, 128)][:, :heads]
+        s0, s1 = jnp.where(first, own, got), jnp.where(first, got, own)
+        log0, log1 = jnp.where(first, own_log, got_log), jnp.where(first, got_log, own_log)
+        p.zero_state[...] = s0
+        p.zero_factor[...] = spread(jnp.exp(log0), heads)
+        chip = spread(jnp.exp(log1), heads)[0:1] * s0 + s1
+        log = log0 + log1
+        log = jnp.concatenate([log, log], axis=0)
+        for j in range(Z):
+            r, q = cell(j)
+            p.z_out[j, :, pl.ds(0, lanes)] = chip[r.start : r.start + 16, q.start : q.start + lanes].astype(BF16)
+            rest = log[:, (j % 2) * part : (j % 2 + 1) * part]
+            pieces = []
+            for _ in range(3):
+                piece = rest.astype(BF16).astype(F32)
+                pieces.append(piece)
+                rest = rest - piece
+            pieces.append(jnp.zeros((16, 128 - 3 * part), F32))
+            p.z_out[j, :, pl.ds(lanes, 128)] = jnp.concatenate(pieces, axis=1).astype(BF16)
+        for k in range(1, Z):
+            cp.send((tag, "z", k), p.z_out.at[lax.rem(z + k, Z)], p.z_in.at[z], to_z[k])
+        p.z_in[z] = p.z_out[z]
+
+    def y_out():
+        for k in range(1, Z):
+            cp.arrived((tag, "z", k), p.z_in.at[lax.rem(z - k + Z, Z)], to_z[k])
+        run = jnp.zeros((16, lanes), F32)
+        logs = jnp.zeros((16, part), F32)
+        for j in range(Z):
+            log = log_of(p.z_in[j, :, pl.ds(lanes, 128)].astype(F32))
+            f = factor(log)
+            p.z_factor[j] = f
+            run = f * run + p.z_in[j, :, pl.ds(0, lanes)].astype(F32)
+            logs = logs + log
+        p.y_in[y, :, pl.ds(0, lanes)] = run
+        p.y_in[y, :, pl.ds(lanes, 128)] = jnp.concatenate([logs, jnp.zeros((16, 128 - part), F32)], axis=1)
+        for k in range(1, Y):
+            cp.send((tag, "y", k), p.y_in.at[y], p.y_in.at[y], to_y[k])
+
+    def z_back():
+        for k in range(1, Y):
+            cp.arrived((tag, "y", k), p.y_in.at[lax.rem(y - k + Y, Y)], to_y[k])
+        run = jnp.zeros((16, lanes), F32)
+        for j in range(Y):
+            f = factor(p.y_in[j, :, pl.ds(lanes, 128)][:, :part])
+            run = jnp.where(j < y, f * run + p.y_in[j, :, pl.ds(0, lanes)], run)
+        for j in range(Z):
+            p.back_out[j] = run.astype(BF16)
+            run = p.z_factor[j] * run + p.z_in[j, :, pl.ds(0, lanes)].astype(F32)
+        for k in range(1, Z):
+            cp.send((tag, "b", k), p.back_out.at[lax.rem(z + k, Z)], p.back_in.at[z], to_z[k])
+        p.back_in[z] = p.back_out[z]
+
+    def core_back():
+        for k in range(1, Z):
+            cp.arrived((tag, "b", k), p.back_in.at[lax.rem(z - k + Z, Z)], to_z[k])
+        rows = [
+            jnp.concatenate([p.back_in[2 * i], p.back_in[2 * i + 1]], axis=1) for i in range(Z // 2)
+        ]
+        zero = jnp.concatenate(rows, axis=0).astype(F32)
+        one = p.zero_factor[0:1, :] * zero + p.zero_state[...]
+        p.core_out[...] = jnp.where(first, one, zero).astype(BF16)
+        cp.send((tag, "core"), p.core_out, prev_ref.at[mine], other)
+        prev_ref[mine, :] = jnp.where(first, zero, one).astype(BF16)
+
+    def done():
+        cp.arrived((tag, "core"), prev_ref.at[theirs], other)
+
+    return [core_out, z_out, y_out, z_back, core_back, done], [*to_z.values(), *to_y.values(), other]
+
+
+N_PREFIX_COPIES = 2 * Z + Y - 1
 
 
 N_WEIGHT_COPIES = 32
@@ -348,25 +428,58 @@
     pl.semaphore_wait(barrier, len(devices))
 
 
-def handoff_body(
-    g_ref, ss_ref, wo_ref, resid_ref, wi_ref, gain_ref, bias_ref, cx_ref, cbc_ref,
-    out_ref, x_ref, bc_ref, step_ref,
-    w_ref, hid_ref, h_ref, opp_ref, right_ref, left_ref, own_ref, sum_r_ref, sum_l_ref,
-    in_l1, in_r1, in_l2, in_r2, ss_in, tail_ref, halo_ref, scale_ref, rs_ref, pre_ref,
-    send_sem, recv_sem, local_sem,
-):
-    rows, width = g_ref.shape
-    heads = step_ref.shape[1]
-    states = bc_ref.shape[1]
+def mixer_body(names, *refs):
+    a = types.SimpleNamespace(**dict(zip(names, refs)))
+    rows, width = a.x_in.shape
+    heads = a.step_in.shape[1]
+    states = a.bc_in.shape[1]
     seq, me = lax.axis_index("seq"), lax.axis_index("head")
     n_seq, n_head = lax.axis_size("seq"), lax.axis_size("head")
     depth = width * n_head
     r, o, l = (lax.rem(me + k, n_head) for k in (1, 2, 3))
     right, opposite, left = ((seq, k) for k in (r, o, l))
     after, before = ((lax.rem(seq + k, n_seq), me) for k in (1, n_seq - 1))
-    cp = Copies(send_sem, recv_sem)
-    steps, partners = weight_steps(cp, wi_ref, w_ref, local_sem)
-    greet([right, left, opposite, after, before, *partners])
+    across = ((1, right), (2, opposite), (3, left))
+    cp = Copies(a.send_sem, a.recv_sem)
+    out_steps, _ = weight_steps(cp, "wo", a.w_out, a.wo, a.local_sem.at[0])
+    steps, _ = weight_steps(cp, "wi", a.w_in, a.wi, a.local_sem.at[1])
+
+    def prefix_of(layer):
+        views = {k: getattr(a, k).at[layer] for k in PREFIX_NAMES}
+        return prefix_steps(
+            cp, ("prefix", layer), heads, a.end, a.total, a.prev.at[layer], types.SimpleNamespace(**views)
+        )
+
+    prefix, partners = prefix_of(0)
+    greet([right, opposite, left, after, before, *partners])
+
+    def turn(work):
+        if work:
+            work.pop(0)()
+
+    turn(out_steps)
+    states_body(a.x_in, a.bc_in, a.step_in, a.code.at[0], a.rate[0:1, :], a.st, a.end, a.total, a.cum)
+    turn(prefix)
+    turn(out_steps)
+    diag = diag_pieces(a.x_in, a.bc_in, a.step_in, a.cum, a.skip[0:1, :], a.own)
+    while prefix:
+        turn(diag)
+        turn(prefix)
+        turn(out_steps)
+    gate_body(a.bc_in, a.cum, a.prev.at[0], a.st, a.own, a.gate, a.norm_gain[...], a.g, a.ss.at[0])
+    for k, device in across:
+        cp.send(("ss", k), a.ss.at[0], a.ss_in.at[k - 1], device)
+    while out_steps:
+        turn(out_steps)
+    turn(steps)
+
+    g_ref, wo_ref, resid_ref, gain_ref, bias_ref = a.g, a.wo, a.resid_in, a.resid_gain, a.bias
+    cx_ref, cbc_ref, out_ref, x_ref, bc_ref, step_ref = a.conv_x, a.conv_bc, a.resid_out, a.x_two, a.bc_two, a.step_two
+    w_ref, hid_ref, h_ref, opp_ref, right_ref, left_ref, own_ref = a.wi, a.hid, a.h, a.opp, a.right, a.left, a.own
+    sum_r_ref, sum_l_ref, in_l1, in_r1, in_l2, in_r2 = a.sum_r, a.sum_l, a.in_l1, a.in_r1, a.in_l2, a.in_r2
+    ss_ref, ss_in, tail_ref, halo_ref, scale_ref, rs_ref, pre_ref = (
+        a.ss.at[0], a.ss_in, a.tail, a.halo, a.scale, a.rs, a.pre
+    )
     chunk = rows // NC
     half = width // 2
     lo, hi = pl.ds(0, half), pl.ds(half, half)
@@ -376,16 +489,12 @@
     def cut(c):
         return pl.ds(c * chunk, chunk)
 
-    steps.pop(0)()
-    for k, device in ((1, right), (2, opposite), (3, left)):
-        cp.send(("ss", k), ss_ref, ss_in.at[k - 1], device)
-
     def product(first, n, dest, store):
         @pl.loop(0, width // tile)
         def _(j):
             at = pl.multiple_of(j * tile, tile)
-            cols = pl.ds(pl.multiple_of(dest * width + at, tile), tile)
-            store(pl.ds(at, tile), bdot(g_ref[pl.ds(first, n), :], wo_ref[:, cols]))
+            weight = wo_ref[dest, pl.ds(j * (Z // 4), Z // 4)].reshape(tile, width)
+            store(pl.ds(at, tile), bdot(g_ref[pl.ds(first, n), :], weight, NT))
 
     def project(k):
         if k % 2:
@@ -421,9 +530,9 @@
         sum_l_ref[q, lo] = left_ref[q, lo].astype(BF16)
         cp.send(("2l", c), sum_l_ref.at[q], in_r2.at[q], left)
 
-    def token_scale():
-        for k, device in ((1, right), (2, opposite), (3, left)):
-            cp.arrived(("ss", k), ss_in.at[k - 1], device)
+    def token_scale(tag, ss_ref, ss_in):
+        for k, device in across:
+            cp.arrived((tag, k), ss_in.at[k - 1], device)
         total = ss_ref[...] + ss_in[0] + ss_in[1] + ss_in[2]
         eighth = jnp.full((8, 128), 0.125, F32)
         column = exact_dot(total, eighth, (((0,), (0,)), ((), ())))
@@ -469,7 +578,7 @@
             k = t - CHUNK_LAG * stage
             if 0 <= k < NC:
                 if work is residual and k == 0:
-                    token_scale()
+                    token_scale("ss", ss_ref, ss_in)
                 work(k if work is project else order[k])
         if steps:
             steps.pop(0)()
@@ -512,40 +621,93 @@
     dt = into(pl.ds(width + states, 128), HALO, rows)
     dt = (dt * rs_ref[pl.ds(HALO, rows), :])[:, :heads] + bias_ref[...]
     step_ref[...] = jnp.maximum(dt, 0.0) + jnp.log(1.0 + jnp.exp(-jnp.abs(dt)))
+
+    states_body(x_ref, bc_ref, step_ref, a.code.at[1], a.rate[1:2, :], a.st, a.end, a.total, a.cum)
+    prefix, _ = prefix_of(1)
+    turn(prefix)
+    diag = diag_pieces(x_ref, bc_ref, step_ref, a.cum, a.skip[1:2, :], a.own)
+    while prefix:
+        turn(diag)
+        turn(prefix)
+    last_body(bc_ref, a.cum, a.prev.at[1], a.st, a.own, a.right, a.ss.at[1])
+    for k, device in across:
+        cp.send(("ss two", k), a.ss.at[1], a.ss_two.at[k - 1], device)
+    token_scale("ss two", a.ss.at[1], a.ss_two)
+    for c in range(NC):
+        q = cut(c)
+        a.mixer_out[q, :] = (a.right[q, :] * scale_ref[q, 0:1]).astype(BF16)
     cp.finish()
 
 
-def handoff(g, ss, w_out_all, resid, w_in, gain, bias, conv_x, conv_bc, heads):
-    rows, width = g.shape
+PREFIX_NAMES = (
+    "pair_out", "pair_in", "zero_state", "zero_factor", "z_out", "z_in", "z_factor", "y_in", "back_out", "back_in", "core_out",
+)
+
+
+def mixer(ins, rows, width, heads, states):
     n_head = lax.axis_size("head")
-    states = conv_bc.shape[1]
-    copies = N_WEIGHT_COPIES + 3 + 1 + 8 * NC
+    n = states // 2
+    lanes = width // 2
+    copies = 2 * N_WEIGHT_COPIES + 2 * N_PREFIX_COPIES + 6 + 1 + 8 * NC
+    outs = {"resid_out": sds(rows, width, dtype=BF16), "mixer_out": sds(rows, width, dtype=BF16)}
+
+    def keep(*shape, dtype=F32):
+        return pltpu.VMEM(shape, dtype)
+
+    small = functools.partial(keep, dtype=BF16)
+    scratch = {
+        "wo": small(Y, Z, CORES, *ins["w_out"].shape),
+        "wi": small(Y, Z, CORES, *ins["w_in"].shape),
+        "hid": small(n_head, rows, width),
+        "h": small(n_head, rows + HALO, width),
+        "opp": small(rows, width),
+        "right": keep(rows, width),
+        "left": keep(rows, width),
+        "own": keep(rows, width),
+        "sum_r": small(rows, width),
+        "sum_l": small(rows, width),
+        "in_l1": small(rows, lanes),
+        "in_r1": small(rows, lanes),
+        "in_l2": small(rows, width),
+        "in_r2": small(rows, width),
+        "g": small(rows, width),
+        "x_two": small(rows, width),
+        "bc_two": small(rows, states),
+        "step_two": keep(rows, heads),
+        "cum": keep(rows, heads),
+        "st": keep(n, width),
+        "end": keep(n, width),
+        "total": keep(8, 128),
+        "prev": small(2, n, width),
+        "ss": keep(2, 8, rows),
+        "ss_in": keep(3, 8, rows),
+        "ss_two": keep(3, 8, rows),
+        "tail": small(n_head, HALO, width),
+        "halo": small(n_head, HALO, width),
+        "scale": keep(rows, 128),
+        "rs": keep(rows + HALO, 128),
+        "pre": keep(rows + HALO, 256),
+        "pair_out": keep(2, n // 2 + 8, width),
+        "pair_in": keep(2, n // 2 + 8, width),
+        "zero_state": keep(2, n // 2, width),
+        "zero_factor": keep(2, 8, width),
+        "z_out": small(2, Z, 16, lanes + 128),
+        "z_in": small(2, Z, 16, lanes + 128),
+        "z_factor": keep(2, Z, 16, lanes),
+        "y_in": keep(2, Y, 16, lanes + 128),
+        "back_out": small(2, Z, 16, lanes),
+        "back_in": small(2, Z, 16, lanes),
+        "core_out": small(2, n // 2, width),
+        "send_sem": pltpu.SemaphoreType.DMA((copies,)),
+        "recv_sem": pltpu.SemaphoreType.DMA((copies,)),
+        "local_sem": pltpu.SemaphoreType.DMA((2,)),
+    }
     return call(
-        handoff_body,
-        (
-            sds(rows, width, dtype=BF16), sds(rows, width, dtype=BF16),
-            sds(rows, states, dtype=BF16), sds(rows, heads),
-        ),
-        (g, ss, w_out_all, resid, w_in, gain, bias, conv_x, conv_bc),
-        [
-            pltpu.VMEM((Y, Z, CORES, *w_in.shape), BF16),
-            pltpu.VMEM((n_head, rows, width), BF16),
-            pltpu.VMEM((n_head, rows + HALO, width), BF16),
-            pltpu.VMEM((rows, width), BF16),
-            *[pltpu.VMEM((rows, width), F32) for _ in range(3)],
-            *[pltpu.VMEM((rows, width), BF16) for _ in range(2)],
-            *[pltpu.VMEM((rows, width // 2), BF16) for _ in range(2)],
-            *[pltpu.VMEM((rows, width), BF16) for _ in range(2)],
-            pltpu.VMEM((3, *ss.shape), F32),
-            *[pltpu.VMEM((n_head, HALO, width), BF16) for _ in range(2)],
-            pltpu.VMEM((rows, 128), F32),
-            pltpu.VMEM((rows + HALO, 128), F32),
-            pltpu.VMEM((rows + HALO, 256), F32),
-            pltpu.SemaphoreType.DMA((copies,)),
-            pltpu.SemaphoreType.DMA((copies,)),
-            pltpu.SemaphoreType.DMA,
-        ],
-        limit=60,
+        functools.partial(mixer_body, (*ins, *outs, *scratch)),
+        tuple(outs.values()),
+        tuple(ins.values()),
+        scratch.values(),
+        limit=62,
         collective_id=1,
         has_side_effects=True,
     )
@@ -566,63 +728,22 @@
     return jax.ShapeDtypeStruct(shape, dtype)
 
 
-def prefix(send, heads):
-    count, wide = send.shape
-    got = lax.all_to_all(send, "seq", 0, 0, tiled=True)
-    width = wide - 128
-    back = call(
-        functools.partial(scan_body, heads),
-        sds(count, width, dtype=BF16),
-        (got,),
-        [pltpu.VMEM((count, width), F32) for _ in range(3)],
-    )
-    return lax.all_to_all(back, "seq", 0, 0, tiled=True)
-
-
-def local_states(x, bc, step, code, rate):
-    rows, heads = step.shape
-    n = bc.shape[1] // 2
-    width = heads * CH
-    return call(
-        states_body,
-        (sds(n // 2, 2 * width + 128, dtype=BF16), sds(n, width), sds(rows, heads)),
-        (x, bc, step, code, rate),
-    )
-
-
-def diagonal(x, bc, step, cum, skip):
-    return call(diag_body, sds(*x.shape), (x, bc, step, cum, skip))
-
-
 def on_device(
     x_in, gate_in, bc_in, step_in, decay_code, decay_rate, skip_gain, norm_gain, w_out, resid_in,
     resid_gain, w_in_x, w_in_bc, w_in_dt, step_time_bias, conv_x, conv_bc,
 ):
     rows, width = x_in.shape
     heads = step_in.shape[1]
-    inner = width * lax.axis_size("head")
-    w_out_all = lax.all_gather(w_out, "seq", axis=1, tiled=True)
     w_in = jnp.concatenate(
         [w_in_x, w_in_bc, jnp.pad(w_in_dt, ((0, 0), (0, 128 - heads)))], axis=1
     )
-
-    send, st, cum = local_states(x_in, bc_in, step_in, decay_code[0], decay_rate[0:1])
-    y = diagonal(x_in, bc_in, step_in, cum, skip_gain[0:1])
-    prev = prefix(send, heads)
-    g, ss = call(
-        gate_body,
-        (sds(rows, width, dtype=BF16), sds(8, rows)),
-        (bc_in, cum, prev, st, y, gate_in, norm_gain[None, :]),
-    )
-    resid_out, x_two, bc_two, step_two = handoff(
-        g, ss, w_out_all, resid_in, w_in, resid_gain[None, :], step_time_bias[None, :], conv_x, conv_bc, heads
-    )
-    send, st, cum = local_states(x_two, bc_two, step_two, decay_code[1], decay_rate[1:2])
-    y = diagonal(x_two, bc_two, step_two, cum, skip_gain[1:2])
-    prev = prefix(send, heads)
-    mixed, ss = call(last_body, (sds(rows, width), sds(8, rows)), (bc_two, cum, prev, st, y))
-    rs = lax.rsqrt(lax.psum(ss[0], "head") / inner + 1e-05)
-    return resid_out, (mixed * rs[:, None]).astype(BF16)
+    ins = {
+        "x_in": x_in, "gate": gate_in, "bc_in": bc_in, "step_in": step_in, "code": decay_code, "rate": decay_rate,
+        "skip": skip_gain, "norm_gain": norm_gain[None, :], "w_out": w_out.T, "resid_in": resid_in,
+        "resid_gain": resid_gain[None, :], "w_in": w_in, "bias": step_time_bias[None, :], "conv_x": conv_x,
+        "conv_bc": conv_bc,
+    }
+    return mixer(ins, rows, width, heads, bc_in.shape[1])
 
 
 def solution(mesh):

time: 306 us -> 206 us (0.67)
  blocking collectives: 56.9 us -> 0 us
  Pallas kernels: 153 us -> 198 us
  waiting for transfers between devices: 31.2 us -> 0 us
  local copies, waits for them, and re-layouts: 26.6 us -> 5.94 us
  between operations: 14.2 us -> 0.66 us
  starting transfers between devices: 12.3 us -> 0 us
  other arithmetic: 10.2 us -> 1.62 us
    all_to_all x2 -> x0, blocking collectives: 47.7 us -> none  [prefix(): got = lax.all_to_all(send, 'seq', 0, 0, tiled=True)]
    pallas_call x9 -> x1, Pallas kernels: 153 us -> 198 us  [call(): pl.pallas_call(body, out_shape=outs, in_specs=[VMEM] * len(args), out_spe...]
    all_gather x1 -> x0, waiting for transfers between devices: 20.3 us -> none  [on_device(): w_out_all = lax.all_gather(w_out, 'seq', axis=1, tiled=True)]
    all_to_all x2 -> x0, starting transfers between devices: 12.2 us -> none  [prefix(): return lax.all_to_all(back, 'seq', 0, 0, tiled=True)]
    all_gather x1 -> x0, local copies, waits for them, and re-layouts: 11.5 us -> none  [on_device(): w_out_all = lax.all_gather(w_out, 'seq', axis=1, tiled=True)]
    all_to_all x2 -> x0, waiting for transfers between devices: 10.2 us -> none  [prefix(): return lax.all_to_all(back, 'seq', 0, 0, tiled=True)]
    psum x1 -> x0, blocking collectives: 9.21 us -> none  [on_device(): rs = lax.rsqrt(lax.psum(ss[0], 'head') / inner + 1e-05)]
    all_to_all x4 -> x0, other arithmetic: 6.78 us -> none  [the longest x2 3.4 us: prefix(): return lax.all_to_all(back, 'seq', 0, 0, tiled=True)]
  transfers between devices with their start and end apart: 3 -> 0, of which waited for: 3 -> 0; matrix products, arithmetic and copies ran while one was open for 5% -> 0% of each run, Pallas kernels for 8% -> 0%
where the time goes in v2:
time: 206 us
  Pallas kernels  198 us (96%)
  local copies, waits for them, and re-layouts  5.94 us (3%)
    pallas_call x1, Pallas kernels, call(): pl.pallas_call(body, out_shape=outs, in_specs=[VMEM] * len(args), out_spe...  198 us
    unnamed x13, local copies, waits for them, and re-layouts  5.94 us

profile of v2, /device:TPU:1, one launch (start us, length us, event | category | flops | bytes accessed | tf_op | source)
XLA Modules:
  0.0 206.2 jit_solution(4910090155260201635)
XLA Ops:
  0.6 0.0 copy-start.3
  0.6 0.7 copy-done.3
  1.3 0.1 copy.19
  1.4 0.0 copy-start.2
  1.4 1.6 fusion.1.refs_11_
  3.0 0.0 copy-done.2
  3.0 0.0 copy-start.1
  3.0 0.8 copy.20.refs_3_
  3.9 0.0 copy-done.1
  3.9 1.0 copy.21.refs_4_
  4.9 197.9 %shard_map.176 = (bf16[512,1024]{1,0:T(8,128)(2,1)}, bf16[512,1024]{1,0:T(8,128)(2,1)}) custom-call(bf16[512,1024]{1,0:T(8,128)(2,1)} %refs_0_.1, bf16[512,1024]{1,0:T(8,128)(2,1)} %refs_1_.1, bf16[512,256]{1,0:T(8,128)(2,1)} %refs_2_.1, f32[512,16]{1,0:T(8,128)} %copy.20.refs_3_, s32[2,512,16]{2,1,0:T(8,128)} %copy.21.refs_4_, f32[2,16]{1,0:T(2,128)} %refs_5_.1, ...), custom_call_target="tpu_custom_call" | custom-call | tf_op jit(solution)/shard_map/pallas_call | solution.py:717
  202.8 0.0 copy-start
  202.8 2.4 %copy.24 = bf16[512,1024]{1,0:T(8,128)(2,1)} copy(bf16[512,1024]{1,0:T(8,128)(2,1)} %get-tuple-element.4) | data formatting | bytes 2097152
  205.2 0.0 copy-done
  205.2 1.0 copy.25
Async XLA Ops:
  0.6 0.7 copy-start.3
  1.4 1.6 copy-start.2
  3.0 0.8 copy-start.1
  202.8 2.4 %copy-start = (bf16[512,1024]{1,0:T(8,128)(2,1)S(1)}, bf16[512,1024]{1,0:T(8,128)(2,1)}, u32[]{:S(2)}) copy-start(bf16[512,1024]{1,0:T(8,128)(2,1)} %get-tuple-element.5) | copy-start | bytes 3145732

commit v3 on v2

--- a/solution.py
+++ b/solution.py
@@ -49,28 +49,24 @@
     return iota((n, n), 0) >= iota((n, n), 1)
 
 
-def states_body(x_ref, bc_ref, step_ref, code_ref, rate, st_ref, end_ref, total_ref, cum_ref):
-    rows, heads = step_ref.shape
-    tri = lower(GROUP).astype(F32)
-    total = state = None
-    for b in range(rows // GROUP):
-        r = pl.ds(b * GROUP, GROUP)
-        decay = -jnp.minimum(code_ref[r, :].astype(F32) * rate, 20.0)
-        cum = exact_dot(tri, decay)
-        cum_ref[r, :] = cum
-        last = cum[GROUP - 1 : GROUP, :]
-        weight = jnp.exp(last - cum) * step_ref[r, :]
-        v = (x_ref[r, :].astype(F32) * spread(weight, heads)).astype(BF16)
-        term = lax.dot_general(
-            bc_ref[r, : bc_ref.shape[1] // 2], v, (((0,), (0,)), ((), ())), preferred_element_type=F32
-        )
-        if state is None:
-            st_ref[...] = term
-            state, total = term, last
-        else:
-            factor = spread(jnp.broadcast_to(jnp.exp(last), (8, heads)), heads)[0:1]
-            state, total = factor * state + term, total + last
-    end_ref[...] = state
+def states_block(b, x_ref, bc_ref, step_ref, code, rate, st_ref, end_ref, total_ref, cum_ref):
+    heads = step_ref.shape[1]
+    r = pl.ds(b * GROUP, GROUP)
+    decay = -jnp.minimum(code.astype(F32).T * rate, 20.0)
+    cum = exact_dot(lower(GROUP).astype(F32), decay)
+    cum_ref[r, :] = cum
+    last = cum[GROUP - 1 : GROUP, :]
+    weight = jnp.exp(last - cum) * step_ref[r, :]
+    v = (x_ref[r, :].astype(F32) * spread(weight, heads)).astype(BF16)
+    term = lax.dot_general(
+        bc_ref[r, : bc_ref.shape[1] // 2], v, (((0,), (0,)), ((), ())), preferred_element_type=F32
+    )
+    if b == 0:
+        st_ref[...] = term
+        return
+    factor = spread(jnp.broadcast_to(jnp.exp(last), (8, heads)), heads)[0:1]
+    end_ref[...] = factor * st_ref[...] + term
+    total = cum_ref[pl.ds(GROUP - 1, 1), :] + last
     wide = jnp.concatenate([total, jnp.zeros((1, 128 - heads), F32)], axis=1)
     total_ref[...] = jnp.broadcast_to(wide, (8, 128))
 
@@ -145,20 +141,24 @@
     return out
 
 
+def squares(v):
+    sq = v * v
+    part = sum(sq[:, k : k + 128] for k in range(128, v.shape[1], 128)) + sq[:, :128]
+    return exact_dot(jnp.ones((8, 128), F32), part, NT)
+
+
 def gate_body(bc_ref, cum_ref, prev_ref, st_ref, y_ref, gate_ref, gain, g_ref, ss_ref):
-    ones = jnp.ones((8, g_ref.shape[1]), F32)
     for r, mixed in mixed_blocks(bc_ref, cum_ref, prev_ref, st_ref, y_ref):
         gate = gate_ref[r, :].astype(F32)
         gated = mixed * (gate / (1.0 + jnp.exp(-gate)))
         g_ref[r, :] = (gated * gain).astype(BF16)
-        ss_ref[:, r] = exact_dot(ones, gated * gated, NT)
+        ss_ref[:, r] = squares(gated)
 
 
 def last_body(bc_ref, cum_ref, prev_ref, st_ref, y_ref, m_ref, ss_ref):
-    ones = jnp.ones((8, m_ref.shape[1]), F32)
     for r, mixed in mixed_blocks(bc_ref, cum_ref, prev_ref, st_ref, y_ref):
         m_ref[r, :] = mixed
-        ss_ref[:, r] = exact_dot(ones, mixed * mixed, NT)
+        ss_ref[:, r] = squares(mixed)
 
 
 NC = 8
@@ -202,12 +202,11 @@
             copy.wait_send()
 
 
-def weight_steps(cp, tag, own, w, local_sem):
+def weight_steps(cp, tag, own, w, local_sem, a_rows):
     y, z, c = place()
     head = lax.axis_index("head")
-    half = own.shape[0] // 2
     f = 1 - 2 * c
-    top, low = pl.ds(0, half), pl.ds(half, half)
+    top, low = pl.ds(0, a_rows), pl.ds(a_rows, own.shape[0] - a_rows)
 
     def at_y(k):
         return lax.rem(y + k * f + 2 * Y, Y)
@@ -225,92 +224,111 @@
     def a_block(kz):
         return w.at[:, at_z(kz), c, top]
 
-    def b_piece(kz):
-        return w.at[y, at_z(kz), c, low]
+    def b_piece(ky, kz):
+        return w.at[at_y(ky), at_z(kz), c, low]
 
     def b_block(ky):
         return w.at[at_y(ky), :, c, low]
 
     def push(name, ref, device):
-        cp.send(name, ref, ref, device)
+        cp.send((tag, *name), ref, ref, device)
+
+    def here(name, ref, device):
+        cp.arrived((tag, *name), ref, device)
 
     def a_share(kz):
-        push((tag, "as", kz), a_block(kz), other)
+        push(("as", kz), a_block(kz), other)
 
     def b_share(ky):
-        push((tag, "bs", ky), b_block(ky), other)
+        push(("bs", ky), b_block(ky), other)
 
     def a_went(way, k):
-        cp.arrived((tag, "az", way, k), a_block(-way * (k + 1)), to_z[way])
+        kz = -way * (k + 1)
+        here(("az", way, k), a_block(kz), to_z[way])
         if k < (3 if way == 1 else 2):
-            push((tag, "az", way, k + 1), a_block(-way * (k + 1)), to_z[way])
-        a_share(-way * (k + 1))
+            push(("az", way, k + 1), a_block(kz), to_z[way])
+        a_share(kz)
 
     def b_went(way, k):
-        cp.arrived((tag, "bz", way, k), b_piece(-way * (k + 1)), to_z[way])
+        kz = -way * (k + 1)
+        here(("bz", way, k), b_piece(0, kz), to_z[way])
         if k < (3 if way == -1 else 2):
-            push((tag, "bz", way, k + 1), b_piece(-way * (k + 1)), to_z[way])
+            push(("bz", way, k + 1), b_piece(0, kz), to_z[way])
+        for along in (-1, 1):
+            push(("by", along, kz), b_piece(0, kz), to_y[along])
+
+    def b_on(kz):
+        here(("by", -1, kz), b_piece(1, kz), to_y[-1])
+        push(("bf", kz), b_piece(1, kz), to_y[-1])
 
     def s0():
         mine = pltpu.make_async_copy(own, w.at[y, z, c], local_sem)
         mine.start()
         for way in (1, -1):
             cp.send((tag, "ay", way, 0), own.at[top], a_piece(0), to_y[way])
-            cp.send((tag, "bz", way, 0), own.at[low], b_piece(0), to_z[way])
+            cp.send((tag, "bz", way, 0), own.at[low], b_piece(0, 0), to_z[way])
+        for way in (-1, 1):
+            cp.send((tag, "by", way, 0), own.at[low], b_piece(0, 0), to_y[way])
         mine.wait()
 
     def s1():
-        cp.arrived((tag, "ay", 1, 0), a_piece(-1), to_y[1])
-        push((tag, "ay", 1, 1), a_piece(-1), to_y[1])
+        here(("ay", 1, 0), a_piece(-1), to_y[1])
+        push(("ay", 1, 1), a_piece(-1), to_y[1])
         b_went(1, 0)
         b_went(-1, 0)
 
     def s2():
-        cp.arrived((tag, "ay", -1, 0), a_piece(1), to_y[-1])
-        cp.arrived((tag, "ay", 1, 1), a_piece(-2), to_y[1])
-        for way in (1, -1):
-            push((tag, "az", way, 0), a_block(0), to_z[way])
-        a_share(0)
+        b_on(0)
         b_went(1, 1)
         b_went(-1, 1)
+        here(("ay", -1, 0), a_piece(1), to_y[-1])
+        here(("ay", 1, 1), a_piece(-2), to_y[1])
+        for way in (1, -1):
+            push(("az", way, 0), a_block(0), to_z[way])
+        a_share(0)
 
     def s3():
         b_went(1, 2)
         b_went(-1, 2)
+        b_on(-1)
+        b_on(1)
         a_went(1, 0)
         a_went(-1, 0)
 
     def s4():
         b_went(-1, 3)
-        for way in (1, -1):
-            push((tag, "by", way, 0), b_block(0), to_y[way])
+        b_on(-2)
+        b_on(2)
         b_share(0)
         a_went(1, 1)
         a_went(-1, 1)
 
     def s5():
+        b_on(-3)
+        b_on(3)
         a_went(1, 2)
         a_went(-1, 2)
-        cp.arrived((tag, "by", -1, 0), b_block(1), to_y[-1])
-        push((tag, "by", -1, 1), b_block(1), to_y[-1])
+
+    def s6():
+        b_on(4)
         b_share(1)
-        cp.arrived((tag, "by", 1, 0), b_block(-1), to_y[1])
+        a_went(1, 3)
+        for kz in range(-3, 5):
+            here(("by", 1, kz), b_piece(-1, kz), to_y[1])
         b_share(-1)
 
-    def s6():
-        a_went(1, 3)
-        cp.arrived((tag, "by", -1, 1), b_block(2), to_y[-1])
+    def s7():
+        for kz in range(-3, 5):
+            here(("bf", kz), b_piece(2, kz), to_y[-1])
         b_share(2)
 
-    def s7():
+    def s8():
         for kz in range(-4, 4):
-            where = w.at[:, lax.rem(z - kz * f + 2 * Z, Z), 1 - c, top]
-            cp.arrived((tag, "as", kz), where, other)
+            here(("as", kz), w.at[:, lax.rem(z - kz * f + 2 * Z, Z), 1 - c, top], other)
         for ky in range(-1, 3):
-            where = w.at[lax.rem(y - ky * f + 2 * Y, Y), :, 1 - c, low]
-            cp.arrived((tag, "bs", ky), where, other)
-
-    return [s0, s1, s2, s3, s4, s5, s6, s7], [*to_y.values(), *to_z.values(), other]
+            here(("bs", ky), w.at[lax.rem(y - ky * f + 2 * Y, Y), :, 1 - c, low], other)
+
+    return [s0, s1, s2, s3, s4, s5, s6, s7, s8]
 
 
 def prefix_steps(cp, tag, heads, end_ref, total_ref, prev_ref, p):
@@ -418,7 +436,7 @@
 N_PREFIX_COPIES = 2 * Z + Y - 1
 
 
-N_WEIGHT_COPIES = 32
+N_WEIGHT_COPIES = 53
 
 
 def greet(devices):
@@ -431,7 +449,7 @@
 def mixer_body(names, *refs):
     a = types.SimpleNamespace(**dict(zip(names, refs)))
     rows, width = a.x_in.shape
-    heads = a.step_in.shape[1]
+    heads = a.step_in.shape[0]
     states = a.bc_in.shape[1]
     seq, me = lax.axis_index("seq"), lax.axis_index("head")
     n_seq, n_head = lax.axis_size("seq"), lax.axis_size("head")
@@ -441,8 +459,8 @@
     after, before = ((lax.rem(seq + k, n_seq), me) for k in (1, n_seq - 1))
     across = ((1, right), (2, opposite), (3, left))
     cp = Copies(a.send_sem, a.recv_sem)
-    out_steps, _ = weight_steps(cp, "wo", a.w_out, a.wo, a.local_sem.at[0])
-    steps, _ = weight_steps(cp, "wi", a.w_in, a.wi, a.local_sem.at[1])
+    out_steps = weight_steps(cp, "wo", a.w_out, a.wo, a.local_sem.at[0], 16)
+    steps = weight_steps(cp, "wi", a.w_in, a.wi, a.local_sem.at[1], 32)
 
     def prefix_of(layer):
         views = {k: getattr(a, k).at[layer] for k in PREFIX_NAMES}
@@ -458,10 +476,18 @@
             work.pop(0)()
 
     turn(out_steps)
-    states_body(a.x_in, a.bc_in, a.step_in, a.code.at[0], a.rate[0:1, :], a.st, a.end, a.total, a.cum)
+    a.step_one[...] = a.step_in[...].T
+
+    def block_states(layer, b, x_ref, bc_ref, step_ref):
+        code = a.code[layer, :, b * GROUP : (b + 1) * GROUP]
+        rate = a.rate[layer : layer + 1, :]
+        states_block(b, x_ref, bc_ref, step_ref, code, rate, a.st, a.end, a.total, a.cum)
+
+    for b in range(rows // GROUP):
+        block_states(0, b, a.x_in, a.bc_in, a.step_one)
     turn(prefix)
     turn(out_steps)
-    diag = diag_pieces(a.x_in, a.bc_in, a.step_in, a.cum, a.skip[0:1, :], a.own)
+    diag = diag_pieces(a.x_in, a.bc_in, a.step_one, a.cum, a.skip[0:1, :], a.own)
     while prefix:
         turn(diag)
         turn(prefix)
@@ -469,9 +495,10 @@
     gate_body(a.bc_in, a.cum, a.prev.at[0], a.st, a.own, a.gate, a.norm_gain[...], a.g, a.ss.at[0])
     for k, device in across:
         cp.send(("ss", k), a.ss.at[0], a.ss_in.at[k - 1], device)
-    while out_steps:
+    while len(out_steps) > 1:
         turn(out_steps)
     turn(steps)
+    turn(out_steps)
 
     g_ref, wo_ref, resid_ref, gain_ref, bias_ref = a.g, a.wo, a.resid_in, a.resid_gain, a.bias
     cx_ref, cbc_ref, out_ref, x_ref, bc_ref, step_ref = a.conv_x, a.conv_bc, a.resid_out, a.x_two, a.bc_two, a.step_two
@@ -483,7 +510,7 @@
     chunk = rows // NC
     half = width // 2
     lo, hi = pl.ds(0, half), pl.ds(half, half)
-    order = [NC - 1 - k for k in range(NC)]
+    order = [NC - 1, *range(NC - 1)]
     tile = 256
 
     def cut(c):
@@ -497,9 +524,10 @@
             store(pl.ds(at, tile), bdot(g_ref[pl.ds(first, n), :], weight, NT))
 
     def project(k):
-        if k % 2:
+        chunks = {0: order[0:1], 1: order[1:2], 2: order[2:4], 4: order[4:6], 6: order[6:8]}.get(k)
+        if chunks is None:
             return
-        first, n = order[k + 1] * chunk, 2 * chunk
+        first, n = chunks[0] * chunk, len(chunks) * chunk
         at = pl.ds(first, n)
 
         def to_opp(cols, p):
@@ -512,7 +540,7 @@
             return store
 
         product(first, n, o, to_opp)
-        for c in (order[k], order[k + 1]):
+        for c in chunks:
             cp.send(("1r", c), opp_ref.at[cut(c), lo], in_l1.at[cut(c)], right)
             cp.send(("1l", c), opp_ref.at[cut(c), hi], in_r1.at[cut(c)], left)
         product(first, n, r, keep(right_ref))
@@ -573,20 +601,6 @@
             cp.send("halo", tail_ref, halo_ref, after)
         scaled(hid_ref, q, c * chunk + HALO, chunk, None)
 
-    for t in range(NC + 4 * CHUNK_LAG):
-        for stage, work in reversed(list(enumerate((project, second_sum, residual, hand_on, complete)))):
-            k = t - CHUNK_LAG * stage
-            if 0 <= k < NC:
-                if work is residual and k == 0:
-                    token_scale("ss", ss_ref, ss_in)
-                work(k if work is project else order[k])
-        if steps:
-            steps.pop(0)()
-    while steps:
-        steps.pop(0)()
-    cp.arrived("halo", halo_ref, after)
-    scaled(halo_ref, pl.ds(0, HALO), 0, HALO, jnp.where(seq == 0, 0.0, 1.0))
-
     def into(cols, at, n):
         total = None
         for k in range(n_head):
@@ -600,36 +614,63 @@
         n = taps.shape[1]
         total = None
         for tap in range(k):
-            v = pre_ref[pl.ds(HALO - k + 1 + tap, rows), :n] * taps[tap : tap + 1, :].astype(F32)
+            v = pre_ref[pl.ds(HALO - k + 1 + tap, GROUP), :n] * taps[tap : tap + 1, :].astype(F32)
             total = v if total is None else total + v
         return (total / (1.0 + jnp.exp(-total))).astype(BF16)
 
-    every = rows + HALO
-
-    def pre(cols):
-        rs = rs_ref[...]
-        pre_ref[...] = (into(cols, 0, every) * jnp.concatenate([rs, rs], axis=1)).astype(BF16).astype(F32)
-
-    @pl.loop(0, width // tile)
-    def _(i):
-        cols = pl.ds(pl.multiple_of(i * tile, tile), tile)
-        pre(cols)
-        x_ref[:, cols] = conv(cx_ref[:, cols], cx_ref.shape[0])
-
-    pre(pl.ds(width, states))
-    bc_ref[...] = conv(cbc_ref[...], cbc_ref.shape[0])
-    dt = into(pl.ds(width + states, 128), HALO, rows)
-    dt = (dt * rs_ref[pl.ds(HALO, rows), :])[:, :heads] + bias_ref[...]
-    step_ref[...] = jnp.maximum(dt, 0.0) + jnp.log(1.0 + jnp.exp(-jnp.abs(dt)))
-
-    states_body(x_ref, bc_ref, step_ref, a.code.at[1], a.rate[1:2, :], a.st, a.end, a.total, a.cum)
+    def second_inputs(b):
+        at, every = b * GROUP, GROUP + HALO
+        r = pl.ds(at, GROUP)
+
+        def pre(cols):
+            rs = rs_ref[pl.ds(at, every), :]
+            both = jnp.concatenate([rs, rs], axis=1)
+            pre_ref[...] = (into(cols, at, every) * both).astype(BF16).astype(F32)
+
+        @pl.loop(0, width // tile)
+        def _(i):
+            cols = pl.ds(pl.multiple_of(i * tile, tile), tile)
+            pre(cols)
+            x_ref[r, cols] = conv(cx_ref[:, cols], cx_ref.shape[0])
+
+        pre(pl.ds(width, states))
+        bc_ref[r, :] = conv(cbc_ref[...], cbc_ref.shape[0])
+        dt = into(pl.ds(width + states, 128), at + HALO, GROUP)
+        dt = (dt * rs_ref[pl.ds(at + HALO, GROUP), :])[:, :heads] + bias_ref[...]
+        step_ref[r, :] = jnp.maximum(dt, 0.0) + jnp.log(1.0 + jnp.exp(-jnp.abs(dt)))
+
+    diag = diag_pieces(x_ref, bc_ref, step_ref, a.cum, a.skip[1:2, :], a.y_two)
+
+    def first_block(t):
+        if t == 4 + 4 * CHUNK_LAG:
+            cp.arrived("halo", halo_ref, after)
+            scaled(halo_ref, pl.ds(0, HALO), 0, HALO, jnp.where(seq == 0, 0.0, 1.0))
+            while steps:
+                turn(steps)
+            second_inputs(0)
+        if t == 5 + 4 * CHUNK_LAG:
+            block_states(1, 0, x_ref, bc_ref, step_ref)
+        if t >= 6 + 4 * CHUNK_LAG:
+            turn(diag)
+
+    for t in range(NC + 4 * CHUNK_LAG):
+        for stage, work in reversed(list(enumerate((project, second_sum, residual, hand_on, complete)))):
+            k = t - CHUNK_LAG * stage
+            if 0 <= k < NC:
+                if work is residual and k == 0:
+                    token_scale("ss", ss_ref, ss_in)
+                work(k if work is project else order[k])
+        if t == 1 or t >= 3:
+            turn(steps)
+        first_block(t)
+    second_inputs(1)
+    block_states(1, 1, x_ref, bc_ref, step_ref)
     prefix, _ = prefix_of(1)
     turn(prefix)
-    diag = diag_pieces(x_ref, bc_ref, step_ref, a.cum, a.skip[1:2, :], a.own)
     while prefix:
         turn(diag)
         turn(prefix)
-    last_body(bc_ref, a.cum, a.prev.at[1], a.st, a.own, a.right, a.ss.at[1])
+    last_body(bc_ref, a.cum, a.prev.at[1], a.st, a.y_two, a.right, a.ss.at[1])
     for k, device in across:
         cp.send(("ss two", k), a.ss.at[1], a.ss_two.at[k - 1], device)
     token_scale("ss two", a.ss.at[1], a.ss_two)
@@ -686,7 +727,9 @@
         "halo": small(n_head, HALO, width),
         "scale": keep(rows, 128),
         "rs": keep(rows + HALO, 128),
-        "pre": keep(rows + HALO, 256),
+        "pre": keep(GROUP + HALO, 256),
+        "y_two": keep(rows, width),
+        "step_one": keep(rows, heads),
         "pair_out": keep(2, n // 2 + 8, width),
         "pair_in": keep(2, n // 2 + 8, width),
         "zero_state": keep(2, n // 2, width),
@@ -738,7 +781,7 @@
         [w_in_x, w_in_bc, jnp.pad(w_in_dt, ((0, 0), (0, 128 - heads)))], axis=1
     )
     ins = {
-        "x_in": x_in, "gate": gate_in, "bc_in": bc_in, "step_in": step_in, "code": decay_code, "rate": decay_rate,
+        "x_in": x_in, "gate": gate_in, "bc_in": bc_in, "step_in": step_in.T, "code": jnp.swapaxes(decay_code, 1, 2), "rate": decay_rate,
         "skip": skip_gain, "norm_gain": norm_gain[None, :], "w_out": w_out.T, "resid_in": resid_in,
         "resid_gain": resid_gain[None, :], "w_in": w_in, "bias": step_time_bias[None, :], "conv_x": conv_x,
         "conv_bc": conv_bc,

time: 206 us -> 174 us (0.84)
  Pallas kernels: 198 us -> 168 us
    pallas_call x1, Pallas kernels: 198 us -> 168 us  [call(): pl.pallas_call(body, out_shape=outs, in_specs=[VMEM] * len(args), out_spe...]
    unnamed x13 -> x7, local copies, waits for them, and re-layouts: 5.94 us -> 4.1 us
where the time goes in v3:
time: 174 us
  Pallas kernels  168 us (97%)
  local copies, waits for them, and re-layouts  4.1 us (2%)
    pallas_call x1, Pallas kernels, call(): pl.pallas_call(body, out_shape=outs, in_specs=[VMEM] * len(args), out_spe...  168 us
    unnamed x7, local copies, waits for them, and re-layouts  4.1 us

profile of v3, /device:TPU:1, one launch (start us, length us, event | category | flops | bytes accessed | tf_op | source)
XLA Modules:
  0.0 174.2 jit_solution(5060984235202459511)
XLA Ops:
  0.6 0.0 copy-start.1
  0.6 0.7 copy-done.1
  1.3 0.1 copy.19
  1.4 1.6 fusion.1.refs_11_
  3.0 167.9 %shard_map.176 = (bf16[512,1024]{1,0:T(8,128)(2,1)}, bf16[512,1024]{1,0:T(8,128)(2,1)}) custom-call(bf16[512,1024]{1,0:T(8,128)(2,1)} %refs_0_.1, bf16[512,1024]{1,0:T(8,128)(2,1)} %refs_1_.1, bf16[512,256]{1,0:T(8,128)(2,1)} %refs_2_.1, f32[16,512]{1,0:T(8,128)} %bitcast.8, s32[2,16,512]{2,1,0:T(8,128)} %bitcast.7, f32[2,16]{1,0:T(2,128)} %refs_5_.1, ...), custom_call_target="tpu_custom_call" | custom-call | tf_op jit(solution)/shard_map/pallas_call | solution.py:760
  170.9 0.0 copy-start
  170.9 2.4 %copy.22 = bf16[512,1024]{1,0:T(8,128)(2,1)} copy(bf16[512,1024]{1,0:T(8,128)(2,1)} %get-tuple-element.4) | data formatting | bytes 2097152
  173.3 0.0 copy-done
  173.3 1.0 copy.23
Async XLA Ops:
  0.6 0.7 copy-start.1
  170.9 2.4 %copy-start = (bf16[512,1024]{1,0:T(8,128)(2,1)S(1)}, bf16[512,1024]{1,0:T(8,128)(2,1)}, u32[]{:S(2)}) copy-start(bf16[512,1024]{1,0:T(8,128)(2,1)} %get-tuple-element.5) | copy-start | bytes 3145732

commit v4 on v3

--- a/solution.py
+++ b/solution.py
@@ -227,9 +227,6 @@
     def b_piece(ky, kz):
         return w.at[at_y(ky), at_z(kz), c, low]
 
-    def b_block(ky):
-        return w.at[at_y(ky), :, c, low]
-
     def push(name, ref, device):
         cp.send((tag, *name), ref, ref, device)
 
@@ -239,8 +236,8 @@
     def a_share(kz):
         push(("as", kz), a_block(kz), other)
 
-    def b_share(ky):
-        push(("bs", ky), b_block(ky), other)
+    def b_share(ky, kz):
+        push(("bs", ky, kz), b_piece(ky, kz), other)
 
     def a_went(way, k):
         kz = -way * (k + 1)
@@ -256,10 +253,18 @@
             push(("bz", way, k + 1), b_piece(0, kz), to_z[way])
         for along in (-1, 1):
             push(("by", along, kz), b_piece(0, kz), to_y[along])
+        b_share(0, kz)
 
     def b_on(kz):
         here(("by", -1, kz), b_piece(1, kz), to_y[-1])
         push(("bf", kz), b_piece(1, kz), to_y[-1])
+        b_share(1, kz)
+        here(("by", 1, kz), b_piece(-1, kz), to_y[1])
+        b_share(-1, kz)
+
+    def b_end(kz):
+        here(("bf", kz), b_piece(2, kz), to_y[-1])
+        b_share(2, kz)
 
     def s0():
         mine = pltpu.make_async_copy(own, w.at[y, z, c], local_sem)
@@ -278,14 +283,15 @@
         b_went(-1, 0)
 
     def s2():
-        b_on(0)
         b_went(1, 1)
         b_went(-1, 1)
         here(("ay", -1, 0), a_piece(1), to_y[-1])
         here(("ay", 1, 1), a_piece(-2), to_y[1])
         for way in (1, -1):
             push(("az", way, 0), a_block(0), to_z[way])
+        b_on(0)
         a_share(0)
+        b_share(0, 0)
 
     def s3():
         b_went(1, 2)
@@ -299,34 +305,35 @@
         b_went(-1, 3)
         b_on(-2)
         b_on(2)
-        b_share(0)
         a_went(1, 1)
         a_went(-1, 1)
+        b_end(0)
 
     def s5():
         b_on(-3)
         b_on(3)
         a_went(1, 2)
         a_went(-1, 2)
+        b_end(-1)
+        b_end(1)
 
     def s6():
         b_on(4)
-        b_share(1)
         a_went(1, 3)
-        for kz in range(-3, 5):
-            here(("by", 1, kz), b_piece(-1, kz), to_y[1])
-        b_share(-1)
+        b_end(-2)
+        b_end(2)
 
     def s7():
-        for kz in range(-3, 5):
-            here(("bf", kz), b_piece(2, kz), to_y[-1])
-        b_share(2)
+        for kz in (-3, 3, 4):
+            b_end(kz)
 
     def s8():
         for kz in range(-4, 4):
             here(("as", kz), w.at[:, lax.rem(z - kz * f + 2 * Z, Z), 1 - c, top], other)
         for ky in range(-1, 3):
-            here(("bs", ky), w.at[lax.rem(y - ky * f + 2 * Y, Y), :, 1 - c, low], other)
+            for kz in range(-3, 5):
+                where = w.at[lax.rem(y - ky * f + 2 * Y, Y), lax.rem(z - kz * f + 2 * Z, Z), 1 - c, low]
+                here(("bs", ky, kz), where, other)
 
     return [s0, s1, s2, s3, s4, s5, s6, s7, s8]
 
@@ -381,7 +388,7 @@
                 rest = rest - piece
             pieces.append(jnp.zeros((16, 128 - 3 * part), F32))
             p.z_out[j, :, pl.ds(lanes, 128)] = jnp.concatenate(pieces, axis=1).astype(BF16)
-        for k in range(1, Z):
+        for k in FAR_FIRST:
             cp.send((tag, "z", k), p.z_out.at[lax.rem(z + k, Z)], p.z_in.at[z], to_z[k])
         p.z_in[z] = p.z_out[z]
 
@@ -390,9 +397,10 @@
             cp.arrived((tag, "z", k), p.z_in.at[lax.rem(z - k + Z, Z)], to_z[k])
         run = jnp.zeros((16, lanes), F32)
         logs = jnp.zeros((16, part), F32)
+        every = log_of(p.z_in[:, :, pl.ds(lanes, 128)].astype(F32).reshape(Z * 16, 128))
+        factors = factor(every)
         for j in range(Z):
-            log = log_of(p.z_in[j, :, pl.ds(lanes, 128)].astype(F32))
-            f = factor(log)
+            log, f = every[16 * j : 16 * j + 16], factors[16 * j : 16 * j + 16]
             p.z_factor[j] = f
             run = f * run + p.z_in[j, :, pl.ds(0, lanes)].astype(F32)
             logs = logs + log
@@ -405,13 +413,14 @@
         for k in range(1, Y):
             cp.arrived((tag, "y", k), p.y_in.at[lax.rem(y - k + Y, Y)], to_y[k])
         run = jnp.zeros((16, lanes), F32)
+        factors = factor(p.y_in[:, :, pl.ds(lanes, 128)].reshape(Y * 16, 128)[:, :part])
         for j in range(Y):
-            f = factor(p.y_in[j, :, pl.ds(lanes, 128)][:, :part])
+            f = factors[16 * j : 16 * j + 16]
             run = jnp.where(j < y, f * run + p.y_in[j, :, pl.ds(0, lanes)], run)
         for j in range(Z):
             p.back_out[j] = run.astype(BF16)
             run = p.z_factor[j] * run + p.z_in[j, :, pl.ds(0, lanes)].astype(F32)
-        for k in range(1, Z):
+        for k in FAR_FIRST:
             cp.send((tag, "b", k), p.back_out.at[lax.rem(z + k, Z)], p.back_in.at[z], to_z[k])
         p.back_in[z] = p.back_out[z]
 
@@ -433,10 +442,11 @@
     return [core_out, z_out, y_out, z_back, core_back, done], [*to_z.values(), *to_y.values(), other]
 
 
+FAR_FIRST = sorted(range(1, Z), key=lambda k: -min(k, Z - k))
 N_PREFIX_COPIES = 2 * Z + Y - 1
 
 
-N_WEIGHT_COPIES = 53
+N_WEIGHT_COPIES = 53 + 28
 
 
 def greet(devices):
@@ -460,7 +470,7 @@
     across = ((1, right), (2, opposite), (3, left))
     cp = Copies(a.send_sem, a.recv_sem)
     out_steps = weight_steps(cp, "wo", a.w_out, a.wo, a.local_sem.at[0], 16)
-    steps = weight_steps(cp, "wi", a.w_in, a.wi, a.local_sem.at[1], 32)
+    steps = weight_steps(cp, "wi", a.wi_own, a.wi, a.local_sem.at[1], 32)
 
     def prefix_of(layer):
         views = {k: getattr(a, k).at[layer] for k in PREFIX_NAMES}
@@ -469,6 +479,18 @@
         )
 
     prefix, partners = prefix_of(0)
+    loads = {
+        name: pltpu.make_async_copy(getattr(a, name + "_hbm"), getattr(a, name), a.local_sem.at[2 + k])
+        for k, name in enumerate(LATE)
+    }
+    for load in loads.values():
+        load.start()
+    a.wi_own[:, pl.ds(0, width)] = a.w_in_x[...]
+    a.wi_own[:, pl.ds(width, states)] = a.w_in_bc[...]
+    dt = a.w_in_dt[...].astype(F32).T
+    dt = jnp.concatenate([dt, jnp.zeros((dt.shape[0], 128 - heads), F32)], axis=1)
+    a.wi_own[:, pl.ds(width + states, 128)] = dt.astype(BF16)
+    a.step_one[...] = a.step_in[...].T
     greet([right, opposite, left, after, before, *partners])
 
     def turn(work):
@@ -476,7 +498,8 @@
             work.pop(0)()
 
     turn(out_steps)
-    a.step_one[...] = a.step_in[...].T
+    loads["x_in"].wait()
+    loads["bc_in"].wait()
 
     def block_states(layer, b, x_ref, bc_ref, step_ref):
         code = a.code[layer, :, b * GROUP : (b + 1) * GROUP]
@@ -492,6 +515,8 @@
         turn(diag)
         turn(prefix)
         turn(out_steps)
+    loads["gate"].wait()
+    loads["resid_in"].wait()
     gate_body(a.bc_in, a.cum, a.prev.at[0], a.st, a.own, a.gate, a.norm_gain[...], a.g, a.ss.at[0])
     for k, device in across:
         cp.send(("ss", k), a.ss.at[0], a.ss_in.at[k - 1], device)
@@ -516,36 +541,30 @@
     def cut(c):
         return pl.ds(c * chunk, chunk)
 
-    def product(first, n, dest, store):
+    def product(dest, store):
         @pl.loop(0, width // tile)
         def _(j):
             at = pl.multiple_of(j * tile, tile)
             weight = wo_ref[dest, pl.ds(j * (Z // 4), Z // 4)].reshape(tile, width)
-            store(pl.ds(at, tile), bdot(g_ref[pl.ds(first, n), :], weight, NT))
-
-    def project(k):
-        chunks = {0: order[0:1], 1: order[1:2], 2: order[2:4], 4: order[4:6], 6: order[6:8]}.get(k)
-        if chunks is None:
-            return
-        first, n = chunks[0] * chunk, len(chunks) * chunk
-        at = pl.ds(first, n)
-
+            store(pl.ds(at, tile), bdot(g_ref[...], weight, NT))
+
+    def project():
         def to_opp(cols, p):
-            opp_ref[at, cols] = p.astype(BF16)
+            opp_ref[:, cols] = p.astype(BF16)
 
         def keep(ref):
             def store(cols, p):
-                ref[at, cols] = p
+                ref[:, cols] = p
 
             return store
 
-        product(first, n, o, to_opp)
-        for c in chunks:
+        product(o, to_opp)
+        for c in order:
             cp.send(("1r", c), opp_ref.at[cut(c), lo], in_l1.at[cut(c)], right)
             cp.send(("1l", c), opp_ref.at[cut(c), hi], in_r1.at[cut(c)], left)
-        product(first, n, r, keep(right_ref))
-        product(first, n, l, keep(left_ref))
-        product(first, n, me, keep(own_ref))
+        product(r, keep(right_ref))
+        product(l, keep(left_ref))
+        product(me, keep(own_ref))
 
     def second_sum(c):
         q = cut(c)
@@ -639,28 +658,29 @@
         dt = (dt * rs_ref[pl.ds(at + HALO, GROUP), :])[:, :heads] + bias_ref[...]
         step_ref[r, :] = jnp.maximum(dt, 0.0) + jnp.log(1.0 + jnp.exp(-jnp.abs(dt)))
 
-    diag = diag_pieces(x_ref, bc_ref, step_ref, a.cum, a.skip[1:2, :], a.y_two)
+    diag = diag_pieces(x_ref, bc_ref, step_ref, a.cum, a.skip[1:2, :], a.right)
 
     def first_block(t):
-        if t == 4 + 4 * CHUNK_LAG:
+        if t == 4 + 3 * CHUNK_LAG:
             cp.arrived("halo", halo_ref, after)
             scaled(halo_ref, pl.ds(0, HALO), 0, HALO, jnp.where(seq == 0, 0.0, 1.0))
             while steps:
                 turn(steps)
             second_inputs(0)
-        if t == 5 + 4 * CHUNK_LAG:
+        if t == 5 + 3 * CHUNK_LAG:
             block_states(1, 0, x_ref, bc_ref, step_ref)
-        if t >= 6 + 4 * CHUNK_LAG:
+        if t >= 6 + 3 * CHUNK_LAG:
             turn(diag)
 
-    for t in range(NC + 4 * CHUNK_LAG):
-        for stage, work in reversed(list(enumerate((project, second_sum, residual, hand_on, complete)))):
+    project()
+    for t in range(NC + 3 * CHUNK_LAG):
+        for stage, work in reversed(list(enumerate((second_sum, residual, hand_on, complete)))):
             k = t - CHUNK_LAG * stage
             if 0 <= k < NC:
                 if work is residual and k == 0:
                     token_scale("ss", ss_ref, ss_in)
-                work(k if work is project else order[k])
-        if t == 1 or t >= 3:
+                work(order[k])
+        if t >= 1:
             turn(steps)
         first_block(t)
     second_inputs(1)
@@ -670,16 +690,33 @@
     while prefix:
         turn(diag)
         turn(prefix)
-    last_body(bc_ref, a.cum, a.prev.at[1], a.st, a.y_two, a.right, a.ss.at[1])
+    last_body(bc_ref, a.cum, a.prev.at[1], a.st, a.right, a.left, a.ss.at[1])
     for k, device in across:
         cp.send(("ss two", k), a.ss.at[1], a.ss_two.at[k - 1], device)
     token_scale("ss two", a.ss.at[1], a.ss_two)
     for c in range(NC):
         q = cut(c)
-        a.mixer_out[q, :] = (a.right[q, :] * scale_ref[q, 0:1]).astype(BF16)
+        a.mixer_out[q, :] = (a.left[q, :] * scale_ref[q, 0:1]).astype(BF16)
     cp.finish()
 
 
+PARTS = 8
+
+
+def place_body(one_ref, two_ref, one_out, two_out, sem):
+    step = one_ref.shape[0] // PARTS
+    copies = [
+        pltpu.make_async_copy(src.at[pl.ds(k * step, step)], dst.at[pl.ds(k * step, step)], sem.at[i, k])
+        for k in range(PARTS)
+        for i, (src, dst) in enumerate(((one_ref, one_out), (two_ref, two_out)))
+    ]
+    for copy in copies:
+        copy.start()
+    for copy in copies:
+        copy.wait()
+
+
+LATE = ("x_in", "bc_in", "gate", "resid_in")
 PREFIX_NAMES = (
     "pair_out", "pair_in", "zero_state", "zero_factor", "z_out", "z_in", "z_factor", "y_in", "back_out", "back_in", "core_out",
 )
@@ -698,7 +735,7 @@
     small = functools.partial(keep, dtype=BF16)
     scratch = {
         "wo": small(Y, Z, CORES, *ins["w_out"].shape),
-        "wi": small(Y, Z, CORES, *ins["w_in"].shape),
+        "wi": small(Y, Z, CORES, ins["w_in_x"].shape[0], width + states + 128),
         "hid": small(n_head, rows, width),
         "h": small(n_head, rows + HALO, width),
         "opp": small(rows, width),
@@ -728,7 +765,8 @@
         "scale": keep(rows, 128),
         "rs": keep(rows + HALO, 128),
         "pre": keep(GROUP + HALO, 256),
-        "y_two": keep(rows, width),
+        "wi_own": small(ins["w_in_x"].shape[0], width + states + 128),
+        **{name: small(*ins[name + "_hbm"].shape) for name in LATE},
         "step_one": keep(rows, heads),
         "pair_out": keep(2, n // 2 + 8, width),
         "pair_in": keep(2, n // 2 + 8, width),
@@ -743,24 +781,25 @@
         "core_out": small(2, n // 2, width),
         "send_sem": pltpu.SemaphoreType.DMA((copies,)),
         "recv_sem": pltpu.SemaphoreType.DMA((copies,)),
-        "local_sem": pltpu.SemaphoreType.DMA((2,)),
+        "local_sem": pltpu.SemaphoreType.DMA((2 + len(LATE),)),
     }
     return call(
         functools.partial(mixer_body, (*ins, *outs, *scratch)),
         tuple(outs.values()),
         tuple(ins.values()),
         scratch.values(),
-        limit=62,
+        limit=58,
+        far=[name.endswith("_hbm") for name in ins],
         collective_id=1,
         has_side_effects=True,
     )
 
 
-def call(body, outs, args, scratch=(), limit=56, **kw):
+def call(body, outs, args, scratch=(), limit=56, far=(), **kw):
     return pl.pallas_call(
         body,
         out_shape=outs,
-        in_specs=[VMEM] * len(args),
+        in_specs=[pl.BlockSpec(memory_space=pl.ANY) if k else VMEM for k in far],
         out_specs=jax.tree.map(lambda _: VMEM, outs),
         scratch_shapes=list(scratch),
         compiler_params=pltpu.CompilerParams(vmem_limit_bytes=limit * 2**20, **kw),
@@ -777,16 +816,22 @@
 ):
     rows, width = x_in.shape
     heads = step_in.shape[1]
-    w_in = jnp.concatenate(
-        [w_in_x, w_in_bc, jnp.pad(w_in_dt, ((0, 0), (0, 128 - heads)))], axis=1
-    )
     ins = {
-        "x_in": x_in, "gate": gate_in, "bc_in": bc_in, "step_in": step_in.T, "code": jnp.swapaxes(decay_code, 1, 2), "rate": decay_rate,
-        "skip": skip_gain, "norm_gain": norm_gain[None, :], "w_out": w_out.T, "resid_in": resid_in,
-        "resid_gain": resid_gain[None, :], "w_in": w_in, "bias": step_time_bias[None, :], "conv_x": conv_x,
+        "x_in_hbm": x_in, "gate_hbm": gate_in, "bc_in_hbm": bc_in, "step_in": step_in.T, "code": jnp.swapaxes(decay_code, 1, 2), "rate": decay_rate,
+        "skip": skip_gain, "norm_gain": norm_gain[None, :], "w_out": w_out.T, "resid_in_hbm": resid_in,
+        "resid_gain": resid_gain[None, :], "w_in_x": w_in_x, "w_in_bc": w_in_bc, "w_in_dt": w_in_dt.T, "bias": step_time_bias[None, :], "conv_x": conv_x,
         "conv_bc": conv_bc,
     }
-    return mixer(ins, rows, width, heads, bc_in.shape[1])
+    outs = mixer(ins, rows, width, heads, bc_in.shape[1])
+    anywhere = pl.BlockSpec(memory_space=pl.ANY)
+    return pl.pallas_call(
+        place_body,
+        out_shape=tuple(sds(*v.shape, dtype=v.dtype) for v in outs),
+        in_specs=[anywhere] * 2,
+        out_specs=(anywhere,) * 2,
+        scratch_shapes=[pltpu.SemaphoreType.DMA((2, PARTS))],
+        compiler_params=pltpu.CompilerParams(vmem_limit_bytes=2**20),
+    )(*outs)
 
 
 def solution(mesh):

time: 174 us -> 171 us (0.983)
    unnamed x7 -> x4, local copies, waits for them, and re-layouts: 4.1 us -> 2.44 us
    pallas_call x1 -> x2, Pallas kernels: 168 us -> 168 us  [the longest x1 166 us: call(): pl.pallas_call(body, out_shape=outs, in_specs=[pl.BlockSpec(memory_space=...]
where the time goes in v4:
time: 171 us
  Pallas kernels  168 us (98%)
  local copies, waits for them, and re-layouts  2.44 us (1%)
    pallas_call x1, Pallas kernels, call(): pl.pallas_call(body, out_shape=outs, in_specs=[pl.BlockSpec(memory_space=...  166 us

profile of v4, /device:TPU:1, one launch (start us, length us, event | category | flops | bytes accessed | tf_op | source)
XLA Modules:
  0.0 171.2 jit_solution(2651838405025636087)
XLA Ops:
  0.6 166.5 %shard_map.176 = (bf16[512,1024]{1,0:T(8,128)(2,1)}, bf16[512,1024]{1,0:T(8,128)(2,1)}) custom-call(bf16[512,1024]{1,0:T(8,128)(2,1)} %refs_0_.1, bf16[512,1024]{1,0:T(8,128)(2,1)} %refs_1_.1, bf16[512,256]{1,0:T(8,128)(2,1)} %refs_2_.1, f32[16,512]{1,0:T(8,128)} %bitcast.9, s32[2,16,512]{2,1,0:T(8,128)} %bitcast.8, f32[2,16]{1,0:T(2,128)} %refs_5_.1, ...), custom_call_target="tpu_custom_call" | custom-call | tf_op jit(solution)/shard_map/pallas_call | solution.py:799
  167.1 0.0 copy-start
  167.1 1.2 copy-done
  168.4 0.0 copy-start.1
  168.4 1.2 copy-done.1
  169.6 1.4 shard_map.177
Async XLA Ops:
  167.1 1.2 copy-start
  168.4 1.2 copy-start.1

commit v5 on v4

--- a/solution.py
+++ b/solution.py
@@ -119,7 +119,7 @@
     ]
 
 
-def mixed_blocks(bc_ref, cum_ref, prev_ref, st_ref, y_ref):
+def mixed_blocks(bc_ref, cum_ref, prev_ref, st_ref, y_ref, grown_ref):
     rows, heads = cum_ref.shape
     n = bc_ref.shape[1] // 2
     out = []
@@ -127,7 +127,6 @@
     for b in range(rows // GROUP):
         r = pl.ds(b * GROUP, GROUP)
         c = bc_ref[r, n:]
-        cum = cum_ref[r, :]
         if b == 0:
             high = prev_ref[...]
             inner = bdot(c, high)
@@ -137,7 +136,7 @@
             state = factor * high.astype(F32) + st_ref[...]
             hi, lo = split_two(state)
             inner = bdot(c, hi) + bdot(c, lo)
-        out.append((r, y_ref[r, :] + inner * spread(jnp.exp(cum), heads)))
+        out.append((r, y_ref[r, :] + inner * grown_ref[r, :]))
     return out
 
 
@@ -147,16 +146,15 @@
     return exact_dot(jnp.ones((8, 128), F32), part, NT)
 
 
-def gate_body(bc_ref, cum_ref, prev_ref, st_ref, y_ref, gate_ref, gain, g_ref, ss_ref):
-    for r, mixed in mixed_blocks(bc_ref, cum_ref, prev_ref, st_ref, y_ref):
-        gate = gate_ref[r, :].astype(F32)
-        gated = mixed * (gate / (1.0 + jnp.exp(-gate)))
+def gate_body(bc_ref, cum_ref, prev_ref, st_ref, y_ref, grown_ref, silu_ref, gain, g_ref, ss_ref):
+    for r, mixed in mixed_blocks(bc_ref, cum_ref, prev_ref, st_ref, y_ref, grown_ref):
+        gated = mixed * silu_ref[r, :]
         g_ref[r, :] = (gated * gain).astype(BF16)
         ss_ref[:, r] = squares(gated)
 
 
-def last_body(bc_ref, cum_ref, prev_ref, st_ref, y_ref, m_ref, ss_ref):
-    for r, mixed in mixed_blocks(bc_ref, cum_ref, prev_ref, st_ref, y_ref):
+def last_body(bc_ref, cum_ref, prev_ref, st_ref, y_ref, grown_ref, m_ref, ss_ref):
+    for r, mixed in mixed_blocks(bc_ref, cum_ref, prev_ref, st_ref, y_ref, grown_ref):
         m_ref[r, :] = mixed
         ss_ref[:, r] = squares(mixed)
 
@@ -511,13 +509,22 @@
     turn(prefix)
     turn(out_steps)
     diag = diag_pieces(a.x_in, a.bc_in, a.step_one, a.cum, a.skip[0:1, :], a.own)
+    def grow():
+        a.left[...] = spread(jnp.exp(a.cum[...]), heads)
+
+    def silu():
+        loads["gate"].wait()
+        gate = a.gate[...].astype(F32)
+        a.right[...] = gate / (1.0 + jnp.exp(-gate))
+        grow()
+
+    diag.append(silu)
     while prefix:
         turn(diag)
         turn(prefix)
         turn(out_steps)
-    loads["gate"].wait()
     loads["resid_in"].wait()
-    gate_body(a.bc_in, a.cum, a.prev.at[0], a.st, a.own, a.gate, a.norm_gain[...], a.g, a.ss.at[0])
+    gate_body(a.bc_in, a.cum, a.prev.at[0], a.st, a.own, a.left, a.right, a.norm_gain[...], a.g, a.ss.at[0])
     for k, device in across:
         cp.send(("ss", k), a.ss.at[0], a.ss_in.at[k - 1], device)
     while len(out_steps) > 1:
@@ -687,10 +694,11 @@
     block_states(1, 1, x_ref, bc_ref, step_ref)
     prefix, _ = prefix_of(1)
     turn(prefix)
+    diag.append(grow)
     while prefix:
         turn(diag)
         turn(prefix)
-    last_body(bc_ref, a.cum, a.prev.at[1], a.st, a.right, a.left, a.ss.at[1])
+    last_body(bc_ref, a.cum, a.prev.at[1], a.st, a.right, a.left, a.left, a.ss.at[1])
     for k, device in across:
         cp.send(("ss two", k), a.ss.at[1], a.ss_two.at[k - 1], device)
     token_scale("ss two", a.ss.at[1], a.ss_two)
@@ -788,7 +796,7 @@
         tuple(outs.values()),
         tuple(ins.values()),
         scratch.values(),
-        limit=58,
+        limit=60,
         far=[name.endswith("_hbm") for name in ins],
         collective_id=1,
         has_side_effects=True,
@@ -830,7 +838,7 @@
         in_specs=[anywhere] * 2,
         out_specs=(anywhere,) * 2,
         scratch_shapes=[pltpu.SemaphoreType.DMA((2, PARTS))],
-        compiler_params=pltpu.CompilerParams(vmem_limit_bytes=2**20),
+        compiler_params=pltpu.CompilerParams(vmem_limit_bytes=62 * 2**20),
     )(*outs)
 
 

time: 171 us -> 232 us (1.36)
  Pallas kernels: 168 us -> 231 us
  local copies, waits for them, and re-layouts: 2.44 us -> 0 us
    pallas_call x1, Pallas kernels: 1.44 us -> 64.8 us  [on_device(): pl.pallas_call(place_body, out_shape=tuple((sds(*v.shape, dtype=v.dtype)...]
    unnamed x4 -> x0, local copies, waits for them, and re-layouts: 2.44 us -> none
where the time goes in v5:
time: 232 us
  Pallas kernels  231 us (100%)
    pallas_call x1, Pallas kernels, call(): pl.pallas_call(body, out_shape=outs, in_specs=[pl.BlockSpec(memory_space=...  166 us
    pallas_call x1, Pallas kernels, on_device(): pl.pallas_call(place_body, out_shape=tuple((sds(*v.shape, dtype=v.dtype)...  64.8 us

profile of v5, /device:TPU:1, one launch (start us, length us, event | category | flops | bytes accessed | tf_op | source)
XLA Modules:
  0.0 231.8 jit_solution(8981655184362076269)
XLA Ops:
  0.6 166.2 %shard_map.176 = (bf16[512,1024]{1,0:T(8,128)(2,1)}, bf16[512,1024]{1,0:T(8,128)(2,1)}) custom-call(bf16[512,1024]{1,0:T(8,128)(2,1)} %refs_0_.1, bf16[512,1024]{1,0:T(8,128)(2,1)} %refs_1_.1, bf16[512,256]{1,0:T(8,128)(2,1)} %refs_2_.1, f32[16,512]{1,0:T(8,128)} %bitcast.9, s32[2,16,512]{2,1,0:T(8,128)} %bitcast.8, f32[2,16]{1,0:T(2,128)} %refs_5_.1, ...), custom_call_target="tpu_custom_call" | custom-call | tf_op jit(solution)/shard_map/pallas_call | solution.py:807
  166.8 64.8 %shard_map.177 = (bf16[512,1024]{1,0:T(8,128)(2,1)}, bf16[512,1024]{1,0:T(8,128)(2,1)}) custom-call(bf16[512,1024]{1,0:T(8,128)(2,1)} %get-tuple-element.4.one_ref, bf16[512,1024]{1,0:T(8,128)(2,1)} %get-tuple-element.5.two_ref), custom_call_target="tpu_custom_call" | custom-call | tf_op jit(solution)/shard_map/pallas_call | solution.py:835
